TPU v7x, 128 devices: a whole 4x4x4 slice. The times are simulated.
128 devices in a mesh: store: 4 (over z), tile: 32 (over y, x, core).
Axes of the slice: x: 4, y: 4, z: 4, core: 2. Of those that a mesh axis runs over, the one named last changes fastest.
Arguments:
- embeddings: bfloat16 [65536, 1024], P(('store', 'tile')), may hold values from -8 to 8
- member_rows: int32 [65536], replicated, may hold values from 0 to 65535, as said below
- cluster_sizes: int32 [8], replicated, may hold values from 2048 to 14336, as said below
- unit_pairs: int32 [128, 1, 3], replicated, may hold values from -1 to 7, as said below
Outputs:
- best_similarity: float32 [65536], P(('store', 'tile'))
Inputs may be any that keep to these rules, and one draw needn't show every extreme that they name: `member_rows`: A permutation of the row ids; clusters lie one after another in this order. Each aligned block of 256 positions holds exactly 2 rows of each device's 512 consecutive row ids. `cluster_sizes`: multiples of 2048 that sum to 65536. `unit_pairs`: each entry is (c, i, j) with i <= j < cluster_sizes[c] // 2048, or (-1, -1, -1) for an empty slot; every such pair of groups of every cluster appears exactly once.
All inputs are finite; a program needn't handle non-finite values.
Results may differ from a plain program's by a relative error of at most 0.00042.
Values may be sent and summed in bfloat16 or wider, within the bound.
A program may use at most 64 MiB of HBM per device.

v0:
```python
import jax
import jax.numpy as jnp
from jax import lax
from jax.sharding import PartitionSpec as P

BLOCK = 256
GROUP_BLOCKS = 8


EPS = 1e-06
FLOOR = -4.0


def compare_unit(operands):
    left_rows, right_rows, left_pos, right_pos = operands
    row_span = min(512, left_rows.shape[0])
    pieces = left_rows.shape[0] // row_span

    def compare_step(col_best, piece_index):
        rows_part = lax.dynamic_slice_in_dim(left_rows, piece_index * row_span, row_span)
        pos_part = lax.dynamic_slice_in_dim(left_pos, piece_index * row_span, row_span)
        scores = lax.dot_general(
            rows_part, right_rows, (((1,), (1,)), ((), ())), preferred_element_type=jnp.float32
        )
        scores = jnp.where(pos_part[:, None] == right_pos[None, :], FLOOR, scores)
        return (jnp.maximum(col_best, jnp.max(scores, axis=0)), jnp.max(scores, axis=1))

    start_best = jnp.full((right_rows.shape[0],), FLOOR, jnp.float32)
    col_best, row_best = lax.scan(compare_step, start_best, jnp.arange(pieces, dtype=jnp.int32))
    return jnp.concatenate([row_best.reshape(-1), col_best])


def shards(embeddings, member_rows, cluster_sizes, unit_pairs):
    devices = lax.axis_size(("store", "tile"))
    myself = lax.axis_index(("store", "tile"))
    rows_dev, feature_width = embeddings.shape
    total_rows = member_rows.shape[0]
    owners = unit_pairs.shape[0]
    units_dev = unit_pairs.shape[1]
    per_block = BLOCK // devices
    group_rows = BLOCK * GROUP_BLOCKS
    both_blocks = 2 * GROUP_BLOCKS
    squares = jnp.sum(jnp.square(embeddings.astype(jnp.float32)), axis=1, keepdims=True)
    unit_rows = (embeddings.astype(jnp.float32) * lax.rsqrt(squares + EPS)).astype(jnp.bfloat16)
    inverse = (
        jnp.zeros((total_rows,), jnp.int32)
        .at[member_rows]
        .set(jnp.arange(total_rows, dtype=jnp.int32))
    )
    my_positions = lax.dynamic_slice_in_dim(inverse, myself * rows_dev, rows_dev)
    by_block = jnp.argsort(my_positions).reshape(total_rows // BLOCK, per_block)
    starts = jnp.cumsum(cluster_sizes) - cluster_sizes
    cluster_ids = jnp.maximum(unit_pairs[:, :, 0], 0)
    first_left = starts[cluster_ids] + jnp.maximum(unit_pairs[:, :, 1], 0) * group_rows
    first_right = starts[cluster_ids] + jnp.maximum(unit_pairs[:, :, 2], 0) * group_rows
    firsts = jnp.stack([first_left, first_right], axis=2)
    offsets = jnp.arange(GROUP_BLOCKS, dtype=jnp.int32)
    block_ids = (firsts[:, :, :, None] // BLOCK + offsets).reshape(owners, units_dev, both_blocks)
    send_rows = by_block[block_ids].reshape(owners, units_dev * both_blocks * per_block)
    outgoing = unit_rows[send_rows]
    slot_count = send_rows.shape[1]
    arrived = lax.all_to_all(outgoing, ("store", "tile"), split_axis=0, concat_axis=0, tiled=True)
    my_units = unit_pairs[myself]
    usable = my_units[:, 0] >= 0
    my_blocks = block_ids[myself]
    positions = my_blocks[:, :, None] * BLOCK + jnp.arange(BLOCK, dtype=jnp.int32)
    my_rows = member_rows[positions]
    sources = my_rows // rows_dev
    earlier = jnp.arange(BLOCK)[:, None] > jnp.arange(BLOCK)[None, :]
    rank_in = jnp.sum(
        ((sources[..., :, None] == sources[..., None, :]) & earlier).astype(jnp.int32), axis=-1
    )
    arrived_slots = arrived.reshape(owners, units_dev, both_blocks, per_block, feature_width)
    unit_idx = jnp.arange(units_dev, dtype=jnp.int32)[:, None, None]
    block_idx = jnp.arange(both_blocks, dtype=jnp.int32)[None, :, None]
    working = arrived_slots[sources, unit_idx, block_idx, rank_in]
    left_rows = working[:, :GROUP_BLOCKS].reshape(units_dev, group_rows, feature_width)
    right_rows = working[:, GROUP_BLOCKS:].reshape(units_dev, group_rows, feature_width)
    pos_flat = positions.reshape(units_dev, 2, group_rows)
    unit_best = lax.map(compare_unit, (left_rows, right_rows, pos_flat[:, 0], pos_flat[:, 1]))
    unit_best = jnp.where(usable[:, None], unit_best, FLOOR).reshape(units_dev, both_blocks, BLOCK)
    back_slots = jnp.full((owners, units_dev, both_blocks, per_block), FLOOR, jnp.float32)
    back_slots = back_slots.at[sources, unit_idx, block_idx, rank_in].set(unit_best)
    returned = lax.all_to_all(
        back_slots.reshape(owners, slot_count),
        ("store", "tile"),
        split_axis=0,
        concat_axis=0,
        tiled=True,
    )
    best_local = (
        jnp.full((rows_dev,), FLOOR, jnp.float32)
        .at[send_rows.reshape(-1)]
        .max(returned.reshape(-1))
    )
    return best_local


def solution(mesh):
    placed = (P(("store", "tile"), None), P(), P(), P())
    return jax.shard_map(
        shards, mesh=mesh, in_specs=placed, out_specs=P(("store", "tile")), check_vma=False
    )
```

profile of v0, /device:TPU:1, one launch (start us, length us, event | category | flops | bytes accessed | tf_op | source)
XLA Modules:
  0.0 588.6 jit_solution(6099393278723111682)
XLA Ops:
  0.0 0.8 reduce-window.9
  0.8 0.7 bitcast_subtract_fusion
  1.5 0.1 add.262
  1.6 1.5 fusion.5
  3.1 0.7 fusion.39
  3.8 5.6 fusion.35
  9.4 0.7 fusion.33
  10.1 0.1 copy.26
  10.2 0.1 reshape.685
  10.3 1.0 compare_select_fusion.1
  11.3 239.6 %scatter_custom_fusion = s32[65536]{0:T(1024)S(1)} fusion(s32[65536]{0:T(1024)S(1)} %compare_select_fusion.1, s32[65536]{0:T(1024)S(1)} %iota.50, s32[]{:T(128)} %constant.48.clone.1), kind=kCustom, calls=%fused_computation.22 | custom fusion | bytes 262148 | tf_op jit(solution)/shard_map/scatter | solution.py:48
  250.9 0.1 dynamic_slice.29
  251.0 3.8 sort.17
  254.8 0.1 reshape.654
  254.9 5.5 gather_fusion
  260.4 0.5 reshape.657
  260.9 0.1 reshape.701
  261.0 0.2 fusion.6
  261.2 18.3 %gather_fusion.2 = bf16[4096,1024]{1,0:T(8,128)(2,1)} fusion(bf16[512,1024]{1,0:T(8,128)(2,1)S(1)} %fusion.6, s32[4096]{0:T(1024)S(1)} %broadcast_clamp_fusion), kind=kCustom, calls=%fused_computation.2 | custom fusion | bytes 16793600 | tf_op jit(solution)/shard_map/gather | solution.py:60
  279.5 12.0 %all-to-all-start = ((bf16[128,32,1024]{2,1,0:T(8,128)(2,1)}), bf16[128,32,1024]{2,1,0:T(8,128)(2,1)}, u32[]{:S(2)}, u32[]{:S(2)}) async-start(bf16[128,32,1024]{2,1,0:T(8,128)(2,1)} %bitcast.108), calls=%async_computation | async-start | bytes 16777216 | tf_op jit(solution)/shard_map/all_to_all | solution.py:62
  291.5 0.2 fusion.25
  291.8 23.0 %gather_fusion.1 = s32[4096]{0:T(1024)S(1)} fusion(s32[65536]{0:T(1024)S(1)} %copy-done, s32[4096]{0:T(1024)S(1)} %broadcast_clamp_fusion.1), kind=kCustom, calls=%fused_computation.1 | custom fusion | bytes 49152 | tf_op jit(solution)/shard_map/gather | solution.py:67
  314.9 0.6 reshape_reshape.3
  315.6 0.1 broadcast_reduce_fusion
  315.7 1.3 convert_reduce_fusion
  317.1 0.1 fusion.9
  317.2 0.1 and_reduce_fusion
  317.4 0.2 dynamic-slice_reduce_fusion
  317.7 72.4 %all-to-all-done = bf16[128,32,1024]{2,1,0:T(8,128)(2,1)} async-done(((bf16[128,32,1024]{2,1,0:T(8,128)(2,1)}), bf16[128,32,1024]{2,1,0:T(8,128)(2,1)}, u32[]{:S(2)}, u32[]{:S(2)}) %all-to-all-start) | async-done | bytes 8388640 | tf_op jit(solution)/shard_map/all_to_all | solution.py:62
  390.1 13.1 %reshape.658 = bf16[128,1,16,2,1024]{4,3,2,1,0:T(2,128)(2,1)} reshape(bf16[128,32,1024]{2,1,0:T(8,128)(2,1)} %all-to-all-done) | data formatting | bytes 16777216 | tf_op jit(solution)/shard_map/reshape | solution.py:73
  403.3 83.8 %gather_fusion.3 = bf16[4096,1024]{1,0:T(8,128)(2,1)} fusion(bf16[128,1,16,2,1024]{4,3,2,1,0:T(2,128)(2,1)} %reshape.658, s32[4096]{0:T(1024)S(1)} %bitcast.106), kind=kCustom, calls=%fused_computation.3 | custom fusion | bytes 16842752 | tf_op jit(solution)/shard_map/gather | solution.py:76
  487.1 5.9 %fusion.37 = (bf16[1,8,256,1024]{3,2,1,0:T(8,128)(2,1)}, bf16[1,8,256,1024]{3,2,1,0:T(8,128)(2,1)}) fusion(bf16[1,16,256,1024]{3,2,1,0:T(8,128)(2,1)} %bitcast.107), kind=kLoop, calls=%fused_computation.102 | loop fusion | bytes 16777216 | tf_op jit(solution)/shard_map/slice | solution.py:78
  493.0 26.2 %while.21 = (s32[]{:T(128)}, f32[2048]{0:T(1024)S(1)}, f32[4,512]{1,0:T(4,128)S(1)}, s32[4]{0:T(128)S(1)}, s32[2048]{0:T(1024)S(1)}, /*index=5*/s32[2048]{0:T(10...) while((s32[]{:T(128)}, f32[2048]{0:T(1024)S(1)}, ...), condition=%wide.region_8.9_spmd.clone, body=%wide.region_5.8_spmd.clone.sunk | while | flops 2151679488 | bytes 5296333 | solution.py:29
  493.0 0.7 dynamic_slice.50
  494.4 5.0 fusion.44
  499.5 0.7 dynamic_slice.50
  500.9 5.0 fusion.44
  506.0 0.7 dynamic_slice.50
  507.5 5.0 fusion.44
  512.6 0.7 dynamic_slice.50
  514.0 5.0 fusion.44
  519.2 15.5 %scatter_custom_fusion.2 = f32[4096]{0:T(1024)S(1)} fusion(s32[4096]{0:T(1024)S(1)} %bitcast.116, f32[4096]{0:T(1024)S(1)} %bitcast.118, f32[]{:T(128)} %constant.47.clone.1), kind=kCustom, calls=%fused_computation.69 | custom fusion | bytes 16388
  534.7 0.7 copy.27
  535.4 12.8 %all-to-all-start.1 = ((f32[128,1,32]{2,1,0:T(1,128)}), f32[128,1,32]{2,1,0:T(1,128)S(1)}, u32[]{:S(2)}, u32[]{:S(2)}) async-start(f32[128,1,32]{2,1,0:T(1,128)} %copy.27), calls=%async_computation.1 | async-start | bytes 131072 | tf_op jit(solution)/shard_map/all_to_all | solution.py:84
  548.3 9.6 %all-to-all-done.1 = f32[128,1,32]{2,1,0:T(1,128)S(1)} async-done(((f32[128,1,32]{2,1,0:T(1,128)}), f32[128,1,32]{2,1,0:T(1,128)S(1)}, u32[]{:S(2)}, u32[]{:S(2)}) %all-to-all-start.1) | async-done | bytes 16416 | tf_op jit(solution)/shard_map/all_to_all | solution.py:84
  557.9 0.5 broadcast.643
  558.4 0.8 reduce.16
  559.3 29.3 %scatter_custom_fusion.1 = f32[512]{0:T(512)} fusion(s32[4096]{0:T(1024)S(1)} %bitcast.117, f32[4096]{0:T(1024)S(1)} %reshape.727, f32[]{:T(128)} %constant.47.clone.1), kind=kCustom, calls=%fused_computation.90 | custom fusion | flops 4096 | bytes 2052 | tf_op jit(solution)/shard_map/scatter-max | solution.py:94
  (60 shorter events, 1.1 us)
Async XLA Ops:
  254.9 6.1 %copy-start.1 = (bf16[512,1024]{1,0:T(8,128)(2,1)S(1)}, bf16[512,1024]{1,0:T(8,128)(2,1)}, u32[]{:S(2)}) copy-start(bf16[512,1024]{1,0:T(8,128)(2,1)} %param.6) | copy-start | bytes 3145732
  279.5 12.3 %copy-start = (s32[65536]{0:T(1024)S(1)}, s32[65536]{0:T(1024)}, u32[]{:S(2)}) copy-start(s32[65536]{0:T(1024)} %param.7) | copy-start | bytes 786436
  279.5 110.6 %all-to-all-start = ((bf16[128,32,1024]{2,1,0:T(8,128)(2,1)}), bf16[128,32,1024]{2,1,0:T(8,128)(2,1)}, u32[]{:S(2)}, u32[]{:S(2)}) async-start(bf16[128,32,1024]{2,1,0:T(8,128)(2,1)} %bitcast.108), calls=%async_computation | async-start | bytes 16777216 | tf_op jit(solution)/shard_map/all_to_all | solution.py:62
  291.8 25.3 %copy-start.4 = (s32[4]{0:T(128)S(1)}, s32[4]{0:T(128)}, u32[]{:S(2)}) copy-start(s32[4]{0:T(128)} %constant.119) | copy-start | bytes 52
  291.8 25.4 %copy-start.3 = (s32[4]{0:T(128)S(1)}, s32[4]{0:T(128)}, u32[]{:S(2)}) copy-start(s32[4]{0:T(128)} %constant.122) | copy-start | bytes 52
  291.8 25.5 %copy-start.2 = (s32[128,1,3]{0,1,2:T(1,128)S(1)}, s32[128,1,3]{0,1,2:T(1,128)}, u32[]{:S(2)}) copy-start(s32[128,1,3]{0,1,2:T(1,128)} %param.9) | copy-start | bytes 4612
  535.4 22.4 %all-to-all-start.1 = ((f32[128,1,32]{2,1,0:T(1,128)}), f32[128,1,32]{2,1,0:T(1,128)S(1)}, u32[]{:S(2)}, u32[]{:S(2)}) async-start(f32[128,1,32]{2,1,0:T(1,128)} %copy.27), calls=%async_computation.1 | async-start | bytes 131072 | tf_op jit(solution)/shard_map/all_to_all | solution.py:84
where the time goes:
time: 590 us; the launch traced here: 589 us
  local copies, waits for them, and re-layouts  412 us (70%)
  waiting for transfers between devices  82 us (14%)
  other arithmetic  46.4 us (8%)
  starting transfers between devices  24.8 us (4%)
  matrix products  20.1 us (3%)
    scatter x1, local copies, waits for them, and re-layouts, shards(): inverse = jnp.zeros((total_rows,), jnp.int32).at[member_rows].set(jnp.ara...  240 us
    gather x1, local copies, waits for them, and re-layouts, shards(): working = arrived_slots[sources, unit_idx, block_idx, rank_in]  83.8 us
    all_to_all x1, waiting for transfers between devices, shards(): lax.all_to_all(outgoing, ('store', 'tile'), split_axis=0, concat_axis=0,...  72.4 us
    another operation x1, other arithmetic, shards(): best_local = jnp.full((rows_dev,), FLOOR, jnp.float32).at[send_rows.resha...  29.3 us
    gather x3, local copies, waits for them, and re-layouts, shards(): my_rows = member_rows[positions]  23 us
    dot_general x4, matrix products, compare_step(): lax.dot_general(rows_part, right_rows, (((1,), (1,)), ((), ())), preferre...  20.1 us
    gather x1, local copies, waits for them, and re-layouts, shards(): outgoing = unit_rows[send_rows]  18.3 us
    unnamed x17, local copies, waits for them, and re-layouts  15.6 us
  transfers between devices with their start and end apart: 2, of which 2 were waited for; matrix products, arithmetic and copies ran while one was open for 4% of the time, Pallas kernels for 0%

commit v1 on v0

v1 whole, which is shorter than its diff:
```python
import jax
import jax.numpy as jnp
from jax import lax
from jax.sharding import PartitionSpec as P

BLOCK = 256
GROUP_BLOCKS = 8
GROUP = BLOCK * GROUP_BLOCKS
AXES = ("store", "tile")
EPS = 1e-06
FLOOR = -4.0


def compare_pair(left, right, same_group):
    span = 512

    def step(col_best, at):
        part = lax.dynamic_slice_in_dim(left, at, span)
        scores = lax.dot_general(part, right, (((1,), (1,)), ((), ())), preferred_element_type=jnp.float32)
        row_ids = at + lax.broadcasted_iota(jnp.int32, scores.shape, 0)
        col_ids = lax.broadcasted_iota(jnp.int32, scores.shape, 1)
        scores = jnp.where((row_ids == col_ids) & same_group, FLOOR, scores)
        return jnp.maximum(col_best, jnp.max(scores, axis=0)), jnp.max(scores, axis=1)

    first = jnp.full((right.shape[0],), FLOOR, jnp.float32)
    col_best, row_best = lax.scan(step, first, jnp.arange(0, left.shape[0], span, dtype=jnp.int32))
    return row_best.reshape(-1), col_best


def shards(embeddings, member_rows, cluster_sizes, unit_pairs):
    devices = lax.axis_size(AXES)
    me = lax.axis_index(AXES)
    rows_dev, width = embeddings.shape
    groups = member_rows.shape[0] // GROUP
    share = GROUP // devices
    owners = unit_pairs.shape[0]

    wide = embeddings.astype(jnp.float32)
    squares = jnp.sum(jnp.square(wide), axis=1, keepdims=True)
    unit = (wide * lax.rsqrt(squares + EPS)).astype(jnp.bfloat16)

    local = member_rows.reshape(-1, BLOCK) - me * rows_dev
    mine = (local >= 0) & (local < rows_dev)
    low = jnp.min(jnp.where(mine, local, rows_dev), axis=1)
    high = jnp.max(jnp.where(mine, local, -1), axis=1)
    order = jnp.stack([low, high], axis=1).reshape(rows_dev)
    pick = order[:, None] == jnp.arange(rows_dev, dtype=jnp.int32)[None, :]
    ordered = lax.dot_general(
        pick.astype(jnp.bfloat16), unit, (((1,), (0,)), ((), ())), preferred_element_type=jnp.float32
    ).astype(jnp.bfloat16)
    by_group = ordered.reshape(groups, share, width)

    first_group = (jnp.cumsum(cluster_sizes) - cluster_sizes) // GROUP
    pairs = unit_pairs[:, 0]
    usable = pairs[:, 0] >= 0
    sides = first_group[jnp.maximum(pairs[:, :1], 0)] + jnp.maximum(pairs[:, 1:], 0)
    outgoing = by_group[sides].reshape(owners, 2 * share, width)
    arrived = lax.all_to_all(outgoing, AXES, split_axis=0, concat_axis=0, tiled=True)
    arrived = arrived.reshape(devices, 2, share, width)
    left = arrived[:, 0].reshape(GROUP, width)
    right = arrived[:, 1].reshape(GROUP, width)
    row_best, col_best = compare_pair(left, right, sides[me, 0] == sides[me, 1])
    best = jnp.stack([row_best.reshape(devices, share), col_best.reshape(devices, share)], axis=1)
    best = jnp.where(usable[me], best, FLOOR).reshape(devices, 2 * share)
    back = lax.all_to_all(best, AXES, split_axis=0, concat_axis=0, tiled=True)
    back = back.reshape(owners * 2, share)
    of_group = sides.reshape(-1)[None, :] == jnp.arange(groups, dtype=jnp.int32)[:, None]
    best_slot = jnp.max(jnp.where(of_group[:, :, None], back[None], FLOOR), axis=1)
    return jnp.max(jnp.where(pick, best_slot.reshape(rows_dev, 1), FLOOR), axis=0)


def solution(mesh):
    placed = (P(AXES, None), P(), P(), P())
    return jax.shard_map(shards, mesh=mesh, in_specs=placed, out_specs=P(AXES), check_vma=False)
```

time: 590 us -> 202 us (0.34)
  local copies, waits for them, and re-layouts: 412 us -> 22.9 us
  other arithmetic: 46.4 us -> 14.3 us
  waiting for transfers between devices: 82 us -> 106 us
    scatter x1 -> x0, local copies, waits for them, and re-layouts: 240 us -> none  [shards(): inverse = jnp.zeros((total_rows,), jnp.int32).at[member_rows].set(jnp.ara...]
    gather x7 -> x2, local copies, waits for them, and re-layouts: 131 us -> 9.28 us  [the longest x1 8.6 us: shards(): outgoing = by_group[sides].reshape(owners, 2 * share, width)]
    another operation x3 -> x2, other arithmetic: 30.2 us -> 0.84 us  [the longest x1 29.3 us: shards(): best_local = jnp.full((rows_dev,), FLOOR, jnp.float32).at[send_rows.resha...]
    all_to_all x2, waiting for transfers between devices: 82 us -> 106 us  [the longest x1 95.9 us: shards(): lax.all_to_all(outgoing, AXES, split_axis=0, concat_axis=0, tiled=True)]
    unnamed x17 -> x1, local copies, waits for them, and re-layouts: 15.6 us -> 0.68 us
    reshape x4 -> x0, local copies, waits for them, and re-layouts: 13.8 us -> none  [the longest x1 13.1 us: shards(): arrived.reshape(owners, units_dev, both_blocks, per_block, feature_width)]
    dot_general x4 -> x5, matrix products: 20.1 us -> 23.4 us  [the longest x4 21.4 us: step(): lax.dot_general(part, right, (((1,), (1,)), ((), ())), preferred_element_...]
  transfers between devices with their start and end apart: 2 -> 2, of which waited for: 2 -> 2; matrix products, arithmetic and copies ran while one was open for 4% -> 1% of each run, Pallas kernels for 0% -> 0%
where the time goes in v1:
time: 202 us; the launch traced here: 201 us
  waiting for transfers between devices  106 us (52%)
  starting transfers between devices  25.1 us (12%)
  matrix products  23.4 us (12%)
  local copies, waits for them, and re-layouts  22.9 us (11%)
  other arithmetic  14.3 us (7%)
  loops' own time  8.44 us (4%)
    all_to_all x1, waiting for transfers between devices, shards(): lax.all_to_all(outgoing, AXES, split_axis=0, concat_axis=0, tiled=True)  95.9 us
    dot_general x4, matrix products, step(): lax.dot_general(part, right, (((1,), (1,)), ((), ())), preferred_element_...  21.4 us
    all_to_all x1, starting transfers between devices, shards(): back = lax.all_to_all(best, AXES, split_axis=0, concat_axis=0, tiled=True)  13.1 us
    all_to_all x1, starting transfers between devices, shards(): lax.all_to_all(outgoing, AXES, split_axis=0, concat_axis=0, tiled=True)  12 us
    all_to_all x1, waiting for transfers between devices, shards(): back = lax.all_to_all(best, AXES, split_axis=0, concat_axis=0, tiled=True)  9.59 us
    gather x1, local copies, waits for them, and re-layouts, shards(): outgoing = by_group[sides].reshape(owners, 2 * share, width)  8.6 us
    another operation x1, loops' own time, compare_pair(): lax.scan(step, first, jnp.arange(0, left.shape[0], span, dtype=jnp.int32))  8.44 us
    slice x1, local copies, waits for them, and re-layouts, shards(): right = arrived[:, 1].reshape(GROUP, width)  6.29 us
  transfers between devices with their start and end apart: 2, of which 2 were waited for; matrix products, arithmetic and copies ran while one was open for 1% of the time, Pallas kernels for 0%

profile of v1, /device:TPU:1, one launch (start us, length us, event | category | flops | bytes accessed | tf_op | source)
XLA Modules:
  0.0 201.1 jit_solution(1637257827816524327)
XLA Ops:
  0.0 0.8 reduce-window.9
  0.8 0.7 and_select_fusion
  1.5 0.7 fusion.14
  2.2 0.7 copy.25
  2.9 4.9 %bitcast_select_fusion = s32[128]{0:T(128)S(1)} fusion(s32[128,3]{0,1:T(4,128)S(1)} %bitcast.47, s32[]{:T(128)} %bitcast.6, s32[]{:T(128)} %bitcast.7, s32[]{:T(128)} %bitcast.8, s32[]{:T(128)} %bitcast.9, s32[]{:T(128)} %bitcast.10, s32[]{:T(128)} %bitcast.12, s32[]{:T(128)} %bitcast.11, s32[]{:T(128)} %bitcast.5), kind=kLoop, calls=%fused_computation.32 | loop fusion | flops 1920 | bytes 1056 | tf_op jit(solution)/shard_map/gather | solution.py:56
  7.8 0.1 copy.18
  7.9 0.1 reshape.114
  8.1 1.0 broadcast_subtract_fusion
  9.1 0.1 sub.18
  9.2 0.2 select_reduce_fusion.3
  9.4 0.1 copy.16
  9.5 0.1 eq.43
  9.6 1.5 fusion.7
  11.2 2.0 %convolution_convert_fusion = bf16[512,1024]{1,0:T(8,128)(2,1)S(1)} fusion(bf16[512,1024]{1,0:T(8,128)(2,1)} %param.6, f32[512]{0:T(512)S(1)} %add_rsqrt_fusion, s32[512]{0:T(512)S(1)} %eq.43), kind=kOutput, calls=%fused_computation.15 | convolution fusion | flops 539230208 | bytes 2101248 | tf_op jit(solution)/shard_map/dot_general | solution.py:48
  13.2 8.6 %gather_fusion = bf16[256,16,1024]{2,1,0:T(8,128)(2,1)} fusion(bf16[32,16,1024]{2,1,0:T(8,128)(2,1)S(1)} %bitcast.41, s32[1024]{0:T(1024)S(1)} %pad_clamp_fusion), kind=kCustom, calls=%fused_computation | custom fusion | bytes 16778240 | tf_op jit(solution)/shard_map/gather | solution.py:57
  21.8 12.0 %all-to-all-start = ((bf16[128,32,1024]{2,1,0:T(8,128)(2,1)}), bf16[128,32,1024]{2,1,0:T(8,128)(2,1)}, u32[]{:S(2)}, u32[]{:S(2)}) async-start(bf16[128,32,1024]{2,1,0:T(8,128)(2,1)} %bitcast.42), calls=%async_computation | async-start | bytes 16777216 | tf_op jit(solution)/shard_map/all_to_all | solution.py:58
  33.8 0.1 copy.17
  33.9 0.1 eq.47
  34.1 0.6 constant_dynamic-slice_fusion.1
  34.6 0.6 constant_dynamic-slice_fusion.2
  36.5 95.9 %all-to-all-done = bf16[128,32,1024]{2,1,0:T(8,128)(2,1)} async-done(((bf16[128,32,1024]{2,1,0:T(8,128)(2,1)}), bf16[128,32,1024]{2,1,0:T(8,128)(2,1)}, u32[]{:S(2)}, u32[]{:S(2)}) %all-to-all-start) | async-done | bytes 8388640 | tf_op jit(solution)/shard_map/all_to_all | solution.py:58
  132.5 6.3 %fusion.13 = (bf16[128,1,16,1024]{3,2,1,0:T(8,128)(2,1)}, bf16[128,1,16,1024]{3,2,1,0:T(8,128)(2,1)}) fusion(bf16[128,2,16,1024]{3,2,1,0:T(8,128)(2,1)} %bitcast.18), kind=kLoop, calls=%fused_computation.51 | loop fusion | bytes 16777216 | tf_op jit(solution)/shard_map/slice | solution.py:61
  138.7 35.5 %while.13 = (s32[]{:T(128)}, f32[2048]{0:T(1024)S(1)}, f32[4,512]{1,0:T(4,128)S(1)}, s32[4]{0:T(128)S(1)}, pred[]{:T(512)}, /*index=5*/bf16[2048,1024]{1,0:T(8,1...) while((s32[]{:T(128)}, f32[2048]{0:T(1024)S(1)}, f32[4,512]{1,0:T(4,128)S(1)}, ...), condition=%wide.region_7.8_spmd.clone, body=%wide.region_4.7_spmd.clone.sunk | while | flops 2152728576 | bytes 5286569 | solution.py:26
  138.7 0.7 dynamic_slice.31
  141.5 0.7 iota_add_fusion.2
  142.2 5.4 %fusion.19 = (f32[512]{0:T(512)S(1)}, f32[2048]{0:T(1024)S(1)}) fusion(s32[512]{0:T(512)S(1)} %iota_add_fusion.2, pred[]{:T(512)} %get-tuple-element.172, bf16[2048,1024]{1,0:T(8,128)(2,1)} %get-tuple-element.174, bf16[2048,1024]{1,0:T(8,128)(2,1)} %get-tuple-element.173, s32[]{:T(128)S(6)} %select_n.83), kind=kOutput, calls=%fused_computation.4.clone.1 | convolution fusion | flops 2152723968 | bytes 5255684 | tf_op jit(solution)/shard_map/while/body/eval_jaxpr/dot_general | solution.py:19
  147.6 0.7 dynamic_slice.31
  150.4 0.7 iota_add_fusion.2
  151.1 5.3 %fusion.19 = (f32[512]{0:T(512)S(1)}, f32[2048]{0:T(1024)S(1)}) fusion(s32[512]{0:T(512)S(1)} %iota_add_fusion.2, pred[]{:T(512)} %get-tuple-element.172, bf16[2048,1024]{1,0:T(8,128)(2,1)} %get-tuple-element.174, bf16[2048,1024]{1,0:T(8,128)(2,1)} %get-tuple-element.173, s32[]{:T(128)S(6)} %select_n.83), kind=kOutput, calls=%fused_computation.4.clone.1 | convolution fusion | flops 2152723968 | bytes 5255684 | tf_op jit(solution)/shard_map/while/body/eval_jaxpr/dot_general | solution.py:19
  156.5 0.7 dynamic_slice.31
  159.2 0.7 iota_add_fusion.2
  159.9 5.4 %fusion.19 = (f32[512]{0:T(512)S(1)}, f32[2048]{0:T(1024)S(1)}) fusion(s32[512]{0:T(512)S(1)} %iota_add_fusion.2, pred[]{:T(512)} %get-tuple-element.172, bf16[2048,1024]{1,0:T(8,128)(2,1)} %get-tuple-element.174, bf16[2048,1024]{1,0:T(8,128)(2,1)} %get-tuple-element.173, s32[]{:T(128)S(6)} %select_n.83), kind=kOutput, calls=%fused_computation.4.clone.1 | convolution fusion | flops 2152723968 | bytes 5255684 | tf_op jit(solution)/shard_map/while/body/eval_jaxpr/dot_general | solution.py:19
  165.4 0.7 dynamic_slice.31
  168.1 0.7 iota_add_fusion.2
  168.8 5.3 %fusion.19 = (f32[512]{0:T(512)S(1)}, f32[2048]{0:T(1024)S(1)}) fusion(s32[512]{0:T(512)S(1)} %iota_add_fusion.2, pred[]{:T(512)} %get-tuple-element.172, bf16[2048,1024]{1,0:T(8,128)(2,1)} %get-tuple-element.174, bf16[2048,1024]{1,0:T(8,128)(2,1)} %get-tuple-element.173, s32[]{:T(128)S(6)} %select_n.83), kind=kOutput, calls=%fused_computation.4.clone.1 | convolution fusion | flops 2152723968 | bytes 5255684 | tf_op jit(solution)/shard_map/while/body/eval_jaxpr/dot_general | solution.py:19
  174.2 0.1 stack_reshape_reshape.3
  174.4 0.1 stack_reshape.3
  174.5 0.6 maximum_select_fusion
  175.1 0.7 copy.21
  175.9 13.1 %all-to-all-start.1 = ((f32[128,1,32]{2,1,0:T(1,128)}), f32[128,1,32]{2,1,0:T(1,128)S(1)}, u32[]{:S(2)}, u32[]{:S(2)}) async-start(f32[128,1,32]{2,1,0:T(1,128)} %copy.21), calls=%async_computation.1 | async-start | bytes 131072 | tf_op jit(solution)/shard_map/all_to_all | solution.py:65
  189.0 9.6 %all-to-all-done.1 = f32[128,1,32]{2,1,0:T(1,128)S(1)} async-done(((f32[128,1,32]{2,1,0:T(1,128)}), f32[128,1,32]{2,1,0:T(1,128)S(1)}, u32[]{:S(2)}, u32[]{:S(2)}) %all-to-all-start.1) | async-done | bytes 16416 | tf_op jit(solution)/shard_map/all_to_all | solution.py:65
  198.6 0.5 broadcast.157
  199.1 0.8 reduce.3
  199.9 0.1 broadcast_in_dim.76
  200.0 0.1 copy.22
  200.1 0.2 select_reduce_fusion.1
  200.2 0.1 broadcast_in_dim.79
  200.3 0.8 select_reduce_fusion
  (19 shorter events, 0.4 us)
Async XLA Ops:
  21.8 110.6 %all-to-all-start = ((bf16[128,32,1024]{2,1,0:T(8,128)(2,1)}), bf16[128,32,1024]{2,1,0:T(8,128)(2,1)}, u32[]{:S(2)}, u32[]{:S(2)}) async-start(bf16[128,32,1024]{2,1,0:T(8,128)(2,1)} %bitcast.42), calls=%async_computation | async-start | bytes 16777216 | tf_op jit(solution)/shard_map/all_to_all | solution.py:58
  175.9 22.7 %all-to-all-start.1 = ((f32[128,1,32]{2,1,0:T(1,128)}), f32[128,1,32]{2,1,0:T(1,128)S(1)}, u32[]{:S(2)}, u32[]{:S(2)}) async-start(f32[128,1,32]{2,1,0:T(1,128)} %copy.21), calls=%async_computation.1 | async-start | bytes 131072 | tf_op jit(solution)/shard_map/all_to_all | solution.py:65

commit v2 on v1

v2 whole, which is shorter than its diff:
```python
import functools

import jax
import jax.numpy as jnp
from jax import lax
from jax.experimental import pallas as pl
from jax.experimental.pallas import tpu as pltpu
from jax.sharding import PartitionSpec as P

BLOCK = 256
GROUP_BLOCKS = 8
GROUP = BLOCK * GROUP_BLOCKS
AXES = ("store", "tile")
EPS = 1e-06
FLOOR = -4.0

MESH = pl.DeviceIdType.MESH
PLANES = 4
SIDE = 4
SLOTS = 8
SHARE = 16
PIECE = 8 * SHARE
CHUNK = SIDE * PIECE
D = 1024
BF16 = jnp.bfloat16
F32 = jnp.float32
I32 = jnp.int32


def compare_pair(left, right, same_group):
    span = 512

    def step(col_best, at):
        part = lax.dynamic_slice_in_dim(left, at, span)
        scores = lax.dot_general(part, right, (((1,), (1,)), ((), ())), preferred_element_type=F32)
        row_ids = at + lax.broadcasted_iota(I32, scores.shape, 0)
        col_ids = lax.broadcasted_iota(I32, scores.shape, 1)
        scores = jnp.where((row_ids == col_ids) & same_group, FLOOR, scores)
        return jnp.maximum(col_best, jnp.max(scores, axis=0)), jnp.max(scores, axis=1)

    first = jnp.full((right.shape[0],), FLOOR, F32)
    col_best, row_best = lax.scan(step, first, jnp.arange(0, left.shape[0], span, dtype=I32))
    return row_best.reshape(-1), col_best


def direct(embeddings, member_rows, cluster_sizes, unit_pairs):
    devices = lax.axis_size(AXES)
    me = lax.axis_index(AXES)
    rows_dev, width = embeddings.shape
    groups = member_rows.size // GROUP
    share = GROUP // devices
    owners = unit_pairs.shape[0]

    wide = embeddings.astype(F32)
    squares = jnp.sum(jnp.square(wide), axis=1, keepdims=True)
    unit = (wide * lax.rsqrt(squares + EPS)).astype(BF16)

    local = member_rows.reshape(-1, BLOCK) - me * rows_dev
    mine = (local >= 0) & (local < rows_dev)
    low = jnp.min(jnp.where(mine, local, rows_dev), axis=1)
    high = jnp.max(jnp.where(mine, local, -1), axis=1)
    order = jnp.stack([low, high], axis=1).reshape(rows_dev)
    pick = order[:, None] == jnp.arange(rows_dev, dtype=I32)[None, :]
    ordered = lax.dot_general(
        pick.astype(BF16), unit, (((1,), (0,)), ((), ())), preferred_element_type=F32
    ).astype(BF16)
    by_group = ordered.reshape(groups, share, width)

    first_group = (jnp.cumsum(cluster_sizes) - cluster_sizes) // GROUP
    pairs = unit_pairs[:, 0]
    usable = pairs[:, 0] >= 0
    sides = first_group[jnp.maximum(pairs[:, :1], 0)] + jnp.maximum(pairs[:, 1:], 0)
    outgoing = by_group[sides].reshape(owners, 2 * share, width)
    arrived = lax.all_to_all(outgoing, AXES, split_axis=0, concat_axis=0, tiled=True)
    arrived = arrived.reshape(devices, 2, share, width)
    left = arrived[:, 0].reshape(GROUP, width)
    right = arrived[:, 1].reshape(GROUP, width)
    row_best, col_best = compare_pair(left, right, sides[me, 0] == sides[me, 1])
    best = jnp.stack([row_best.reshape(devices, share), col_best.reshape(devices, share)], axis=1)
    best = jnp.where(usable[me], best, FLOOR).reshape(devices, 2 * share)
    back = lax.all_to_all(best, AXES, split_axis=0, concat_axis=0, tiled=True)
    back = back.reshape(owners * 2, share)
    of_group = sides.reshape(-1)[None, :] == jnp.arange(groups, dtype=I32)[:, None]
    best_slot = jnp.max(jnp.where(of_group[:, :, None], back[None], FLOOR), axis=1)
    return jnp.max(jnp.where(pick, best_slot.reshape(rows_dev, 1), FLOOR), axis=0)


def prepare_kernel(clusters, sizes_ref, emb_ref, members_ref, rows_ref, ids_ref, clus_ref, fits_ref, group_at):
    me = lax.axis_index("store") * (2 * SIDE * SIDE) + lax.axis_index("tile")
    rows_dev = emb_ref.shape[0]
    counts = [sizes_ref[c] // GROUP for c in range(clusters)]
    way = lax.broadcasted_iota(I32, (128, 128), 0) * 128 + lax.broadcasted_iota(I32, (128, 128), 1)
    loads = jnp.full((128, 128), counts[0], I32)
    for c in range(1, clusters):
        plane = lax.shift_right_logical(way, 2 * (c - 1)) & 3
        loads += lax.shift_left(jnp.full((128, 128), counts[c], I32), plane * 8)
    most = loads & 255
    for p in range(1, PLANES):
        most = jnp.maximum(most, lax.shift_right_logical(loads, 8 * p) & 255)
    chosen = jnp.min(most * 16384 + way)
    fits_ref[0] = (chosen // 16384 <= SLOTS).astype(I32)
    groups = PLANES * SLOTS
    for d in range(groups):
        group_at[d] = 0
        clus_ref[d] = -1
    used = [jnp.int32(0)] * PLANES
    start = jnp.int32(0)
    for c in range(clusters):
        plane = jnp.int32(0) if c == 0 else lax.shift_right_logical(chosen, 2 * (c - 1)) & 3
        offset = jnp.int32(0)
        for p in range(PLANES):
            offset = jnp.where(plane == p, used[p], offset)

        def put(i, carry, c=c, plane=plane, offset=offset, start=start):
            at = jnp.minimum(plane * SLOTS + offset + i, groups - 1)
            group_at[at] = jnp.minimum(start + i, groups - 1)
            clus_ref[at] = c
            return carry

        lax.fori_loop(0, counts[c], put, 0)
        for p in range(PLANES):
            used[p] = jnp.where(plane == p, used[p] + counts[c], used[p])
        start = start + counts[c]

    def ids_of(d, carry):
        at = pl.multiple_of(group_at[d] * GROUP_BLOCKS, GROUP_BLOCKS)
        local = members_ref[pl.ds(at, GROUP_BLOCKS), :] - me * rows_dev
        mine = (local >= 0) & (local < rows_dev)
        low = jnp.min(jnp.where(mine, local, rows_dev), axis=1, keepdims=True)
        high = jnp.max(jnp.where(mine, local, -1), axis=1, keepdims=True)
        to = pl.multiple_of(d * SHARE, SHARE)
        ids_ref[pl.ds(to, 8), :] = jnp.broadcast_to(low, (8, 128))
        ids_ref[pl.ds(to + 8, 8), :] = jnp.broadcast_to(high, (8, 128))
        return carry

    lax.fori_loop(0, groups, ids_of, 0)
    wide = emb_ref[...].astype(F32)
    squares = jnp.sum(wide * wide, axis=1, keepdims=True)
    unit = (wide * lax.rsqrt(squares + EPS)).astype(BF16)
    pick = ids_ref[:, :1] == lax.broadcasted_iota(I32, (rows_dev, rows_dev), 1)
    picked = lax.dot_general(
        jnp.where(pick, 1.0, 0.0).astype(BF16), unit, (((1,), (0,)), ((), ())), preferred_element_type=F32
    )
    rows_ref[...] = picked.astype(BF16)


def prepare(embeddings, member_rows, cluster_sizes):
    rows_dev, width = embeddings.shape
    vmem = pl.BlockSpec(memory_space=pltpu.VMEM)
    smem = pl.BlockSpec(memory_space=pltpu.SMEM)
    groups = PLANES * SLOTS
    return pl.pallas_call(
        functools.partial(prepare_kernel, cluster_sizes.shape[0]),
        out_shape=(
            jax.ShapeDtypeStruct((rows_dev, width), BF16),
            jax.ShapeDtypeStruct((rows_dev, 128), I32),
            jax.ShapeDtypeStruct((groups,), I32),
            jax.ShapeDtypeStruct((1,), I32),
        ),
        in_specs=[smem, vmem, vmem],
        out_specs=(vmem, vmem, smem, smem),
        scratch_shapes=[pltpu.SMEM((groups,), I32)],
        compiler_params=pltpu.CompilerParams(vmem_limit_bytes=32 * 2**20),
        name="prepare",
    )(cluster_sizes, embeddings, member_rows.reshape(-1, BLOCK))


def plane_kernel(
    clus_ref, src, ids_ref, out_ref,
    zbuf, erow, ecol, fbuf, hbuf, racc, cacc, fcacc, fsend, hsend,
    rrow, rcol, brow, bcol, zout, fin,
    zs, zr, es, er, ec, gs, fr, hr, ss, sr,
    rs, rr, rc, bs, br, ts, tr,
):
    z = lax.axis_index("store")
    tile = lax.axis_index("tile")
    y, x, k = tile // 8, (tile // 2) % 4, tile % 2

    def dev(dz, dy, dx, dk):
        return (dz, dy * 8 + dx * 2 + dk)

    def row_first(cy, cx):
        step = lax.rem(cx - cy + 4, 4)
        return (step == 1) | ((step == 2) & (cy < 2))

    diagonal = y == x
    by_row = row_first(y, x)

    def copy(start, from_, to, ssem, rsem, dz, dy, dx, dk):
        mine = (dz == z) & (dy == y) & (dx == x) & (dk == k)
        far = pltpu.make_async_remote_copy(from_, to, ssem, rsem, device_id=dev(dz, dy, dx, dk), device_id_type=MESH)

        @pl.when(jnp.logical_not(mine))
        def _():
            if start:
                far.start()
            else:
                far.wait_send()

        if start:

            @pl.when(mine)
            def _():
                pltpu.make_async_copy(from_, to, rsem).start()

    def arrive(ref, sem):
        pltpu.make_async_copy(ref, ref, sem).wait()

    for ref in (rrow, rcol):
        ref[...] = jnp.full(ref.shape, FLOOR, F32)
    for ref in (racc, cacc, fcacc):
        ref[...] = jnp.full(ref.shape, FLOOR, F32)
    for ref in (fsend, hsend):
        ref[...] = jnp.full(ref.shape, FLOOR, F32)

    barrier = pltpu.get_barrier_semaphore()

    def greet(i, carry):
        @pl.when((i // 2 != y) | (i % 2 != k))
        def _():
            pl.semaphore_signal(barrier, inc=1, device_id=dev(z, i // 2, x, i % 2), device_id_type=MESH)

        @pl.when(i // 2 != x)
        def _():
            pl.semaphore_signal(barrier, inc=1, device_id=dev(z, y, i // 2, i % 2), device_id_type=MESH)

        return carry

    lax.fori_loop(0, 8, greet, 0)
    for step in range(1, PLANES):
        pl.semaphore_signal(barrier, inc=1, device_id=dev(lax.rem(z + step, 4), y, x, k), device_id_type=MESH)
    pl.semaphore_wait(barrier, 7 + 6 + 3)

    def planes(start):
        def one(c, carry):
            to = lax.rem(z - c + 4, 4)
            copy(
                start, src.at[pl.ds(pl.multiple_of(to * PIECE, PIECE), PIECE)],
                zbuf.at[pl.ds(pl.multiple_of(c * PIECE, PIECE), PIECE)], zs.at[c], zr.at[c], to, y, x, k,
            )
            return carry

        lax.fori_loop(0, PLANES, one, 0)

    def exchange(start, c):
        def one(i, carry):
            b, j = i // 2, i % 2
            piece = zbuf.at[pl.ds(pl.multiple_of(c * PIECE + i * SHARE, SHARE), SHARE)]
            in_row = pl.multiple_of(c * PIECE + (2 * y + k) * SHARE, SHARE)
            in_col = pl.multiple_of(c * PIECE + (2 * x + k) * SHARE, SHARE)
            copy(start, piece, erow.at[pl.ds(in_row, SHARE)], es.at[c, 0, i], er.at[c], z, b, x, j)
            copy(start, piece, ecol.at[pl.ds(in_col, SHARE)], es.at[c, 1, i], ec.at[c], z, y, b, j)
            return carry

        lax.fori_loop(0, 8, one, 0)

    def gather(start, c):
        at = pl.multiple_of(c * PIECE, PIECE)

        def one(i, carry):
            cx = lax.rem(x + 1 + i, 4)
            to = pl.multiple_of(c * CHUNK + x * PIECE, PIECE)
            full = (cx == y) | row_first(y, cx)

            @pl.when(full)
            def _():
                copy(start, erow.at[pl.ds(at, PIECE)], fbuf.at[pl.ds(to, PIECE)], gs.at[c, 0, i, 0], fr.at[c], z, y, cx, k)

            @pl.when(jnp.logical_not(full) & (k == 1))
            def _():
                for h in range(2):
                    copy(
                        start, erow.at[pl.ds(at + h * 64, 64)], hbuf.at[pl.ds(to + h * 64, 64)],
                        gs.at[c, 0, i, h], hr.at[c], z, y, cx, h,
                    )

            cy = lax.rem(y + 1 + i, 4)
            to_col = pl.multiple_of(c * CHUNK + y * PIECE, PIECE)

            @pl.when(cy == x)
            def _():
                copy(start, ecol.at[pl.ds(at, PIECE)], hbuf.at[pl.ds(to_col, PIECE)], gs.at[c, 1, i, 0], hr.at[c], z, cy, x, 1 - k)

            @pl.when((cy != x) & jnp.logical_not(row_first(cy, x)))
            def _():
                copy(start, ecol.at[pl.ds(at, PIECE)], fbuf.at[pl.ds(to_col, PIECE)], gs.at[c, 1, i, 0], fr.at[c], z, cy, x, k)

            @pl.when((cy != x) & row_first(cy, x) & (k == 0))
            def _():
                for h in range(2):
                    copy(
                        start, ecol.at[pl.ds(at + h * 64, 64)], hbuf.at[pl.ds(to_col + h * 64, 64)],
                        gs.at[c, 1, i, h], hr.at[c], z, cy, x, h,
                    )

            return carry

        lax.fori_loop(0, SIDE, one, 0)

    def sibling(start, c):
        def one(i, carry):
            half = hbuf.at[pl.ds(pl.multiple_of(c * CHUNK + i * PIECE + k * 64, 64), 64)]
            copy(start, half, half, ss.at[c, i], sr.at[c], z, y, x, 1 - k)
            return carry

        lax.fori_loop(0, SIDE, one, 0)

    def begin_exchange(c):
        arrive(zbuf.at[pl.ds(c * PIECE, PIECE)], zr.at[c])
        exchange(True, c)

    def begin_gather(c):
        arrive(erow.at[pl.ds(c * PIECE, PIECE)], er.at[c])
        arrive(ecol.at[pl.ds(c * PIECE, PIECE)], ec.at[c])
        gather(True, c)

    planes(True)
    begin_exchange(0)

    def feed(c, carry):
        begin_exchange(c + 1)
        begin_gather(c)
        return carry

    lax.fori_loop(0, PLANES - 1, feed, 0)
    begin_gather(PLANES - 1)

    first_slot = jnp.where(diagonal | by_row, 2 * y, 2 * x) + k
    other_slot = jnp.where(diagonal, 2 * y + 1 - k, jnp.where(by_row, 2 * x, 2 * y + 1))
    together = clus_ref[z * SLOTS + first_slot] == clus_ref[z * SLOTS + other_slot]

    def scores_of(left, i, right, j):
        a = left[pl.ds(pl.multiple_of(i * CHUNK, CHUNK), CHUNK), :]
        b = right[pl.ds(pl.multiple_of(j * CHUNK, CHUNK), CHUNK), :]
        return lax.dot_general(a, b, (((1,), (1,)), ((), ())), preferred_element_type=F32)

    def keep(scores, i, j, col, ok):
        over = scores[:, :128]
        for n in range(1, CHUNK // 128):
            over = jnp.maximum(over, scores[:, n * 128 : (n + 1) * 128])
        down = jnp.max(scores.reshape(CHUNK // 8, 8, CHUNK), axis=0)
        if ok is not None:
            over = jnp.where(ok, over, FLOOR)
            down = jnp.where(ok, down, FLOOR)
        at = pl.ds(pl.multiple_of(i * CHUNK, CHUNK), CHUNK)
        racc[at, :] = jnp.maximum(racc[at, :], over)
        col[j] = jnp.maximum(col[j], down)

    def compute(c, carry):
        here = pl.ds(pl.multiple_of(c * CHUNK, CHUNK), CHUNK)

        @pl.when(diagonal)
        def _():
            arrive(hbuf.at[here], hr.at[c])

        @pl.when(jnp.logical_not(diagonal))
        def _():
            arrive(hbuf.at[pl.ds(pl.multiple_of(c * CHUNK, 256), 256)], hr.at[c])
            sibling(True, c)

        arrive(fbuf.at[here], fr.at[c])

        @pl.when(diagonal)
        def _():
            def own(t, inner):
                keep(scores_of(fbuf, c, fbuf, t), c, t, fcacc, None)
                return inner

            lax.fori_loop(0, c, own, 0)
            scores = scores_of(fbuf, c, fbuf, c)
            same = lax.broadcasted_iota(I32, scores.shape, 0) == lax.broadcasted_iota(I32, scores.shape, 1)
            keep(jnp.where(same, FLOOR, scores), c, c, fcacc, None)

        @pl.when(jnp.logical_not(diagonal))
        def _():
            arrive(hbuf.at[pl.ds(pl.multiple_of(c * CHUNK, 256), 256)], sr.at[c])

        def cross(t, inner):
            i = jnp.where(t <= c, c, t - c - 1)
            j = jnp.where(t <= c, t, c)
            wanted = jnp.logical_not(diagonal) | ((k == 0) & (i < 2)) | ((k == 1) & (j >= 2))

            @pl.when(wanted)
            def _():
                keep(scores_of(fbuf, i, hbuf, j), i, j, cacc, together)

            return inner

        lax.fori_loop(0, 2 * c + 1, cross, 0)
        return carry

    lax.fori_loop(0, PLANES, compute, 0)

    for c in range(PLANES):
        down = jnp.max(cacc[c], axis=0, keepdims=True)
        own = jnp.max(fcacc[c], axis=0, keepdims=True)
        for s in range(SIDE):
            lanes = slice(s * 128, (s + 1) * 128)
            at = c * CHUNK + s * PIECE
            over = jnp.max(racc[at : at + PIECE, :].T, axis=0, keepdims=True)
            fsend[s, c : c + 1, :] = jnp.maximum(over, own[:, lanes])
            hsend[s, c : c + 1, :] = down[:, lanes]

    def results(start):
        def one(s, carry):
            to_row = diagonal | by_row

            @pl.when(to_row)
            def _():
                copy(start, fsend.at[s], rrow.at[x, 0], rs.at[0, s], rr.at[x, 0], z, y, s, k)

            @pl.when(jnp.logical_not(to_row))
            def _():
                copy(start, fsend.at[s], rcol.at[y, 0], rs.at[0, s], rc.at[y, 0], z, s, x, k)

            @pl.when(diagonal)
            def _():
                copy(start, hsend.at[s], rcol.at[y, 0], rs.at[1, s], rc.at[y, 0], z, s, x, 1 - k)

            @pl.when(jnp.logical_not(diagonal) & by_row)
            def _():
                copy(start, hsend.at[s], rcol.at[y, k], rs.at[1, s], rc.at[y, k], z, s, x, 0)

            @pl.when(jnp.logical_not(to_row))
            def _():
                copy(start, hsend.at[s], rrow.at[x, k], rs.at[1, s], rr.at[x, k], z, y, s, 1)

            return carry

        lax.fori_loop(0, SIDE, one, 0)

    results(True)

    def results_here(i, carry):
        full = (i == y) | row_first(y, i)

        @pl.when(full | (k == 1))
        def _():
            arrive(rrow.at[i, 0], rr.at[i, 0])

        @pl.when(jnp.logical_not(full) & (k == 1))
        def _():
            arrive(rrow.at[i, 1], rr.at[i, 1])

        part = (i != x) & row_first(i, x)

        @pl.when(jnp.logical_not(part) | (k == 0))
        def _():
            arrive(rcol.at[i, 0], rc.at[i, 0])

        @pl.when(part & (k == 0))
        def _():
            arrive(rcol.at[i, 1], rc.at[i, 1])

        return carry

    lax.fori_loop(0, SIDE, results_here, 0)
    for ref in (rrow, rcol):
        total = ref[0, 0]
        for i in range(SIDE):
            for j in range(2):
                if i or j:
                    total = jnp.maximum(total, ref[i, j])
        ref[0, 0] = total

    def unexchange(start):
        def one(i, carry):
            b, j = i // 2, i % 2
            copy(start, rrow.at[0, 0], brow.at[2 * y + k], bs.at[0, i], br.at[0], z, b, x, j)
            copy(start, rcol.at[0, 0], bcol.at[2 * x + k], bs.at[1, i], br.at[1], z, y, b, j)
            return carry

        lax.fori_loop(0, 8, one, 0)

    unexchange(True)
    arrive(brow, br.at[0])
    arrive(bcol, br.at[1])
    for c in range(PLANES):
        from_row = jnp.concatenate([brow[s, c : c + 1, :] for s in range(SLOTS)], axis=0)
        from_col = jnp.concatenate([bcol[s, c : c + 1, :] for s in range(SLOTS)], axis=0)
        from_row = pltpu.roll(from_row, lax.rem(128 - (2 * y + k) * SHARE, 128), 1)
        from_col = pltpu.roll(from_col, lax.rem(128 - (2 * x + k) * SHARE, 128), 1)
        zout[c] = jnp.maximum(from_row, from_col)

    def unplanes(start):
        def one(c, carry):
            copy(start, zout.at[c], fin.at[z], ts.at[c], tr.at[z], lax.rem(z + c, 4), y, x, k)
            return carry

        lax.fori_loop(0, PLANES, one, 0)

    unplanes(True)
    for p in range(PLANES):
        arrive(fin.at[p], tr.at[p])

    rows = PLANES * PIECE
    spread = jnp.broadcast_to(fin[...].reshape(PLANES * SLOTS, 1, 128), (PLANES * SLOTS, SHARE, 128)).reshape(rows, 128)
    lane = lax.broadcasted_iota(I32, (rows, 128), 1)
    sub = lax.rem(lax.broadcasted_iota(I32, (rows, 128), 0), SHARE)
    value = jnp.max(jnp.where(lane == sub, spread, FLOOR), axis=1, keepdims=True)
    pick = ids_ref[:, :1] == lax.broadcasted_iota(I32, (rows, rows), 1)
    out_ref[...] = jnp.max(jnp.where(pick, value, FLOOR), axis=0, keepdims=True)

    planes(False)

    def sent(c, carry):
        exchange(False, c)
        gather(False, c)

        @pl.when(jnp.logical_not(diagonal))
        def _():
            sibling(False, c)

        return carry

    lax.fori_loop(0, PLANES, sent, 0)
    results(False)
    unexchange(False)
    unplanes(False)


def by_planes(rows, ids, clus):
    vmem = pl.BlockSpec(memory_space=pltpu.VMEM)
    smem = pl.BlockSpec(memory_space=pltpu.SMEM)
    dma = pltpu.SemaphoreType.DMA
    best = pl.pallas_call(
        plane_kernel,
        out_shape=jax.ShapeDtypeStruct((1, rows.shape[0]), F32),
        in_specs=[smem, vmem, vmem],
        out_specs=vmem,
        scratch_shapes=[
            pltpu.VMEM((PLANES * PIECE, D), BF16),
            pltpu.VMEM((PLANES * PIECE, D), BF16),
            pltpu.VMEM((PLANES * PIECE, D), BF16),
            pltpu.VMEM((PLANES * CHUNK, D), BF16),
            pltpu.VMEM((PLANES * CHUNK, D), BF16),
            pltpu.VMEM((PLANES * CHUNK, 128), F32),
            pltpu.VMEM((PLANES, 8, CHUNK), F32),
            pltpu.VMEM((PLANES, 8, CHUNK), F32),
            pltpu.VMEM((SIDE, 8, 128), F32),
            pltpu.VMEM((SIDE, 8, 128), F32),
            pltpu.VMEM((SIDE, 2, 8, 128), F32),
            pltpu.VMEM((SIDE, 2, 8, 128), F32),
            pltpu.VMEM((SLOTS, 8, 128), F32),
            pltpu.VMEM((SLOTS, 8, 128), F32),
            pltpu.VMEM((PLANES, 8, 128), F32),
            pltpu.VMEM((PLANES, 8, 128), F32),
            dma((PLANES,)), dma((PLANES,)),
            dma((PLANES, 2, 8)), dma((PLANES,)), dma((PLANES,)),
            dma((PLANES, 2, SIDE, 2)), dma((PLANES,)), dma((PLANES,)),
            dma((PLANES, SIDE)), dma((PLANES,)),
            dma((2, SIDE)), dma((SIDE, 2)), dma((SIDE, 2)),
            dma((2, 8)), dma((2,)),
            dma((PLANES,)), dma((PLANES,)),
        ],
        compiler_params=pltpu.CompilerParams(
            collective_id=0, has_side_effects=True, vmem_limit_bytes=40 * 2**20
        ),
        name="by_planes",
    )(clus, rows, ids)
    return best.reshape(-1)


def shards(embeddings, member_rows, cluster_sizes, unit_pairs):
    rows, ids, clus, fits = prepare(embeddings, member_rows, cluster_sizes)
    return lax.cond(
        fits[0] > 0,
        lambda: by_planes(rows, ids, clus),
        lambda: direct(embeddings, member_rows, cluster_sizes, unit_pairs),
    )


def solution(mesh):
    placed = (P(AXES, None), P(), P(), P())
    return jax.shard_map(shards, mesh=mesh, in_specs=placed, out_specs=P(AXES), check_vma=False)
```

time: 202 us -> 105 us (0.52)
  waiting for transfers between devices: 106 us -> 0 us
  Pallas kernels: 0 us -> 102 us
  starting transfers between devices: 25.1 us -> 0 us
  matrix products: 23.4 us -> 0 us
  local copies, waits for them, and re-layouts: 22.9 us -> 1.61 us
  other arithmetic: 14.3 us -> 0 us
  loops' own time: 8.44 us -> 0.2 us
    all_to_all x2 -> x0, waiting for transfers between devices: 106 us -> none  [the longest x1 95.9 us: shards(): lax.all_to_all(outgoing, AXES, split_axis=0, concat_axis=0, tiled=True)]
    pallas_call x0 -> x2, Pallas kernels: none -> 102 us  [the longest x1 94.3 us: by_planes(): pl.pallas_call(plane_kernel, out_shape=jax.ShapeDtypeStruct((1, rows.shap...]
    all_to_all x2 -> x0, starting transfers between devices: 25.1 us -> none  [the longest x1 13.1 us: shards(): back = lax.all_to_all(best, AXES, split_axis=0, concat_axis=0, tiled=True)]
    dot_general x5 -> x0, matrix products: 23.4 us -> none  [the longest x4 21.4 us: step(): lax.dot_general(part, right, (((1,), (1,)), ((), ())), preferred_element_...]
    gather x2 -> x0, local copies, waits for them, and re-layouts: 9.28 us -> none  [the longest x1 8.6 us: shards(): outgoing = by_group[sides].reshape(owners, 2 * share, width)]
    another operation x1, loops' own time: 8.44 us -> 0.2 us  [shards(): lax.cond(fits[0] > 0, lambda: by_planes(rows, ids, clus), lambda: direct(...]
    slice x1 -> x0, local copies, waits for them, and re-layouts: 6.29 us -> none  [shards(): right = arrived[:, 1].reshape(GROUP, width)]
    gather x2 -> x0, other arithmetic: 4.95 us -> none  [the longest x1 4.94 us: shards(): first_group[jnp.maximum(pairs[:, :1], 0)] + jnp.maximum(pairs[:, 1:], 0)]
  transfers between devices with their start and end apart: 2 -> 0, of which waited for: 2 -> 0; matrix products, arithmetic and copies ran while one was open for 1% -> 0% of each run, Pallas kernels for 0% -> 0%
where the time goes in v2:
time: 105 us
  Pallas kernels  102 us (97%)
  local copies, waits for them, and re-layouts  1.61 us (2%)
    pallas_call x1, Pallas kernels, by_planes(): pl.pallas_call(plane_kernel, out_shape=jax.ShapeDtypeStruct((1, rows.shap...  94.3 us
    pallas_call x1, Pallas kernels, prepare(): pl.pallas_call(functools.partial(prepare_kernel, cluster_sizes.shape[0]),...  8.02 us

profile of v2, /device:TPU:1, one launch (start us, length us, event | category | flops | bytes accessed | tf_op | source)
XLA Modules:
  0.0 104.8 jit_solution(17202038057643727191)
XLA Ops:
  0.0 1.0 reshape.111.members_ref
  1.0 8.0 %prepare.1 = (bf16[512,1024]{1,0:T(8,128)(2,1)S(1)}, s32[512,128]{1,0:T(8,128)S(1)}, s32[32]{0:T(128)S(1)}, s32[1]{0:T(128)}) custom-call(s32[8]{0:T(128)} %sizes_ref.1, bf16[512,1024]{1,0:T(8,128)(2,1)} %emb_ref.1, s32[256,256]{1,0:T(8,128)S(1)} %reshape.111.members_ref), custom_call_target="tpu_custom_call" | custom-call | tf_op jit(solution)/shard_map/prepare/pallas_call | solution.py:152
  9.7 94.5 %conditional.1 = (f32[512]{0:T(512)S(1)}) conditional(s32[]{:T(128)} %bitcast.22, (s32[65536]{0:T(1024)}, s32[8]{0:T(128)}, s32[128,1,3]{0,1,2:T(1,128)}, bf16[512,1024]{1,0:T(8,128)(2,1)}) %tuple.15, (s32[32]{0:T(128)S(1)}, bf16[512,1024]{1,0:T(8,128)(2,1)S(1)}, s32[512,128]{1,0:T(8,128)S(1)}) %tuple.16), branch_computations={%region_0.11_spmd, %region_11.12_spmd} | conditional | flops 2695124480 | bytes 68931608 | solution.py:566
  9.9 94.3 %by_planes.1 = f32[1,512]{1,0:T(1,128)S(1)} custom-call(s32[32]{0:T(128)S(1)} %get-tuple-element.64.clus_ref, bf16[512,1024]{1,0:T(8,128)(2,1)S(1)} %get-tuple-element.65.src, s32[512,128]{1,0:T(8,128)S(1)} %get-tuple-element.66.ids_ref), custom_call_target="tpu_custom_call" | custom-call | tf_op jit(solution)/shard_map/cond/branch_1_fun/by_planes/pallas_call | solution.py:526
  104.2 0.6 copy.41

commit v3 on v1

v3 whole, which is shorter than its diff:
```python
import functools

import jax
import jax.numpy as jnp
from jax import lax
from jax.experimental import pallas as pl
from jax.experimental.pallas import tpu as pltpu
from jax.sharding import PartitionSpec as P

BLOCK = 256
GROUP_BLOCKS = 8
GROUP = BLOCK * GROUP_BLOCKS
AXES = ("store", "tile")
EPS = 1e-06
FLOOR = -4.0

MESH = pl.DeviceIdType.MESH
PLANES = 4
SIDE = 4
SLOTS = 8
SHARE = 16
PIECE = 8 * SHARE
CHUNK = SIDE * PIECE
HALF = PIECE // 2
D = 1024
BF16 = jnp.bfloat16
F32 = jnp.float32
I32 = jnp.int32


def compare_pair(left, right, same_group):
    span = 512

    def step(col_best, at):
        part = lax.dynamic_slice_in_dim(left, at, span)
        scores = lax.dot_general(part, right, (((1,), (1,)), ((), ())), preferred_element_type=F32)
        row_ids = at + lax.broadcasted_iota(I32, scores.shape, 0)
        col_ids = lax.broadcasted_iota(I32, scores.shape, 1)
        scores = jnp.where((row_ids == col_ids) & same_group, FLOOR, scores)
        return jnp.maximum(col_best, jnp.max(scores, axis=0)), jnp.max(scores, axis=1)

    first = jnp.full((right.shape[0],), FLOOR, F32)
    col_best, row_best = lax.scan(step, first, jnp.arange(0, left.shape[0], span, dtype=I32))
    return row_best.reshape(-1), col_best


def direct(embeddings, member_rows, cluster_sizes, unit_pairs):
    devices = lax.axis_size(AXES)
    me = lax.axis_index(AXES)
    rows_dev, width = embeddings.shape
    groups = member_rows.size // GROUP
    share = GROUP // devices
    owners = unit_pairs.shape[0]

    wide = embeddings.astype(F32)
    squares = jnp.sum(jnp.square(wide), axis=1, keepdims=True)
    unit = (wide * lax.rsqrt(squares + EPS)).astype(BF16)

    local = member_rows.reshape(-1, BLOCK) - me * rows_dev
    mine = (local >= 0) & (local < rows_dev)
    low = jnp.min(jnp.where(mine, local, rows_dev), axis=1)
    high = jnp.max(jnp.where(mine, local, -1), axis=1)
    order = jnp.stack([low, high], axis=1).reshape(rows_dev)
    pick = order[:, None] == jnp.arange(rows_dev, dtype=I32)[None, :]
    ordered = lax.dot_general(
        pick.astype(BF16), unit, (((1,), (0,)), ((), ())), preferred_element_type=F32
    ).astype(BF16)
    by_group = ordered.reshape(groups, share, width)

    first_group = (jnp.cumsum(cluster_sizes) - cluster_sizes) // GROUP
    pairs = unit_pairs[:, 0]
    usable = pairs[:, 0] >= 0
    sides = first_group[jnp.maximum(pairs[:, :1], 0)] + jnp.maximum(pairs[:, 1:], 0)
    outgoing = by_group[sides].reshape(owners, 2 * share, width)
    arrived = lax.all_to_all(outgoing, AXES, split_axis=0, concat_axis=0, tiled=True)
    arrived = arrived.reshape(devices, 2, share, width)
    left = arrived[:, 0].reshape(GROUP, width)
    right = arrived[:, 1].reshape(GROUP, width)
    row_best, col_best = compare_pair(left, right, sides[me, 0] == sides[me, 1])
    best = jnp.stack([row_best.reshape(devices, share), col_best.reshape(devices, share)], axis=1)
    best = jnp.where(usable[me], best, FLOOR).reshape(devices, 2 * share)
    back = lax.all_to_all(best, AXES, split_axis=0, concat_axis=0, tiled=True)
    back = back.reshape(owners * 2, share)
    of_group = sides.reshape(-1)[None, :] == jnp.arange(groups, dtype=I32)[:, None]
    best_slot = jnp.max(jnp.where(of_group[:, :, None], back[None], FLOOR), axis=1)
    return jnp.max(jnp.where(pick, best_slot.reshape(rows_dev, 1), FLOOR), axis=0)


def prepare_kernel(clusters, sizes_ref, emb_ref, members_ref, rows_ref, ids_ref, clus_ref, fits_ref, group_at, low_ref, high_ref, picked_ref):
    me = lax.axis_index("store") * (2 * SIDE * SIDE) + lax.axis_index("tile")
    rows_dev = emb_ref.shape[0]
    blocks = members_ref.shape[0] // 2
    local = [members_ref[pl.ds(h, blocks, stride=2), :] - me * rows_dev for h in range(2)]
    mine = [(part >= 0) & (part < rows_dev) for part in local]
    low = [jnp.where(ok, part, rows_dev) for ok, part in zip(mine, local)]
    high = [jnp.where(ok, part, -1) for ok, part in zip(mine, local)]
    low = jnp.min(jnp.minimum(*low), axis=1, keepdims=True)
    high = jnp.max(jnp.maximum(*high), axis=1, keepdims=True)
    low_ref[...] = jnp.broadcast_to(low, (blocks, 128))
    high_ref[...] = jnp.broadcast_to(high, (blocks, 128))
    wide = emb_ref[...].astype(F32)
    squares = jnp.sum(wide * wide, axis=1, keepdims=True)
    unit = (wide * lax.rsqrt(squares + EPS)).astype(BF16)
    column = lax.broadcasted_iota(I32, (blocks, rows_dev), 1)
    for h, wanted in enumerate((low, high)):
        pick = jnp.where(wanted == column, 1.0, 0.0).astype(BF16)
        picked_ref[h * blocks : (h + 1) * blocks, :] = lax.dot_general(
            pick, unit, (((1,), (0,)), ((), ())), preferred_element_type=F32
        )

    counts = [sizes_ref[c] // GROUP for c in range(clusters)]
    way = lax.broadcasted_iota(I32, (128, 128), 0) * 128 + lax.broadcasted_iota(I32, (128, 128), 1)
    loads = jnp.full((128, 128), counts[0], I32)
    for c in range(1, clusters):
        plane = lax.shift_right_logical(way, 2 * (c - 1)) & 3
        loads += lax.shift_left(jnp.full((128, 128), counts[c], I32), plane * 8)
    most = loads & 255
    for p in range(1, PLANES):
        most = jnp.maximum(most, lax.shift_right_logical(loads, 8 * p) & 255)
    chosen = jnp.min(most * 16384 + way)
    fits_ref[0] = (chosen // 16384 <= SLOTS).astype(I32)
    groups = PLANES * SLOTS
    for d in range(groups):
        group_at[d] = 0
        clus_ref[d] = -1
    used = [jnp.int32(0)] * PLANES
    start = jnp.int32(0)
    for c in range(clusters):
        plane = jnp.int32(0) if c == 0 else lax.shift_right_logical(chosen, 2 * (c - 1)) & 3
        offset = jnp.int32(0)
        for p in range(PLANES):
            offset = jnp.where(plane == p, used[p], offset)

        def put(i, carry, c=c, plane=plane, offset=offset, start=start):
            at = jnp.minimum(plane * SLOTS + offset + i, groups - 1)
            group_at[at] = jnp.minimum(start + i, groups - 1)
            clus_ref[at] = c
            return carry

        lax.fori_loop(0, counts[c], put, 0)
        for p in range(PLANES):
            used[p] = jnp.where(plane == p, used[p] + counts[c], used[p])
        start = start + counts[c]

    for d in range(groups):
        at = pl.multiple_of(group_at[d] * GROUP_BLOCKS, GROUP_BLOCKS)
        ids_ref[d * SHARE : d * SHARE + 8, :] = low_ref[pl.ds(at, 8), :]
        ids_ref[d * SHARE + 8 : d * SHARE + 16, :] = high_ref[pl.ds(at, 8), :]
        lower = picked_ref[pl.ds(at, 8), :]
        upper = picked_ref[pl.ds(pl.multiple_of(at + 256, 8), 8), :]
        rows_ref[d * SHARE : (d + 1) * SHARE, :] = jnp.concatenate([lower, upper], axis=0).astype(BF16)


def prepare(embeddings, member_rows, cluster_sizes):
    rows_dev, width = embeddings.shape
    vmem = pl.BlockSpec(memory_space=pltpu.VMEM)
    smem = pl.BlockSpec(memory_space=pltpu.SMEM)
    groups = PLANES * SLOTS
    return pl.pallas_call(
        functools.partial(prepare_kernel, cluster_sizes.shape[0]),
        out_shape=(
            jax.ShapeDtypeStruct((rows_dev, width), BF16),
            jax.ShapeDtypeStruct((rows_dev, 128), I32),
            jax.ShapeDtypeStruct((groups,), I32),
            jax.ShapeDtypeStruct((1,), I32),
        ),
        in_specs=[smem, vmem, vmem],
        out_specs=(vmem, vmem, smem, smem),
        scratch_shapes=[
            pltpu.SMEM((groups,), I32),
            pltpu.VMEM((member_rows.size // BLOCK, 128), I32),
            pltpu.VMEM((member_rows.size // BLOCK, 128), I32),
            pltpu.VMEM((rows_dev, width), F32),
        ],
        compiler_params=pltpu.CompilerParams(vmem_limit_bytes=32 * 2**20),
        name="prepare",
    )(cluster_sizes, embeddings, member_rows.reshape(-1, BLOCK // 2))


def plane_kernel(
    clus_ref, src, ids_ref, out_ref,
    zbuf, erow, ecol, fbuf, hbuf, racc, cacc, fcacc, fsend, hsend,
    rrow, rcol, brow, bcol, zout, fin,
    zs, zr, es, er, ec, gs, vs, fr, hr, ss, sr,
    rs, rr, bs, br, ts,
):
    z = lax.axis_index("store")
    tile = lax.axis_index("tile")
    y, x, k = tile // 8, (tile // 2) % 4, tile % 2

    def far(from_, to, ssem, rsem, dz, dy, dx, dk):
        pltpu.make_async_remote_copy(
            from_, to, ssem, rsem, device_id=(dz, dy * 8 + dx * 2 + dk), device_id_type=MESH
        ).start()

    def near(from_, to, rsem):
        pltpu.make_async_copy(from_, to, rsem).start()

    def arrive(ref, sem):
        pltpu.make_async_copy(ref, ref, sem).wait()

    def row_first(cy, cx):
        step = (cx - cy) & 3
        return (step == 1) | ((step == 2) & (cy < 2))

    diagonal = y == x
    across = jnp.logical_not(diagonal)
    by_row = row_first(y, x)
    in_row, in_col = 2 * y + k, 2 * x + k

    for ref in (rrow, rcol):
        ref[...] = jnp.full(ref.shape, FLOOR, F32)

    barrier = pltpu.get_barrier_semaphore()

    def greet(dz, dy, dx, dk):
        pl.semaphore_signal(barrier, inc=1, device_id=(dz, dy * 8 + dx * 2 + dk), device_id_type=MESH)

    for n in range(1, 8):
        i = (in_row + n) & 7
        greet(z, i // 2, x, i & 1)
    for n in range(1, SIDE):
        for core in range(2):
            greet(z, y, (x + n) & 3, core)
        greet((z + n) & 3, y, x, k)
    pl.semaphore_wait(barrier, 7 + 6 + 3)

    def hop(c):
        return (0, 1, 3, 2)[c]

    def chunk(c):
        return pl.ds(c * PIECE if isinstance(c, int) else pl.multiple_of(c * PIECE, PIECE), PIECE)

    def exchange(c):
        arrive(zbuf.at[chunk(c)], zr.at[c])
        row_at = pl.ds(pl.multiple_of(c * PIECE + in_row * SHARE, SHARE), SHARE)
        col_at = pl.ds(pl.multiple_of(c * PIECE + in_col * SHARE, SHARE), SHARE)

        def piece(i):
            return zbuf.at[pl.ds(pl.multiple_of(c * PIECE + i * SHARE, SHARE), SHARE)]

        for n in range(1, 8):
            i = (in_row + n) & 7
            far(piece(i), erow.at[row_at], es, er.at[c], z, i // 2, x, i & 1)
            i = (in_col + n) & 7
            far(piece(i), ecol.at[col_at], es, ec.at[c], z, y, i // 2, i & 1)
        near(piece(in_row), erow.at[row_at], er.at[c])
        near(piece(in_col), ecol.at[col_at], ec.at[c])

    lines = []
    for role, (ebuf, esem, line, pos) in enumerate(((erow, er, y, x), (ecol, ec, x, y))):
        mine = (pos - line) & 3
        special = k == role
        wide = line < 2
        goals = []
        for n in (1, 3, 0):
            r = (mine + n) & 3
            p = (pos + n) & 3
            whole = (r == 1) | ((r == 2) & wide) | ((r == 0) & special)
            halves = ((r == 3) | ((r == 2) & jnp.logical_not(wide))) & jnp.logical_not(special)
            goals.append((n, p, whole, halves))
        lines.append((role, ebuf, esem, pos, goals))

    def gather(c):
        for role, ebuf, esem, pos, goals in lines:
            arrive(ebuf.at[chunk(c)], esem.at[c])
            to = c * SIDE + pos
            for n, p, whole, halves in goals:
                py, px = (y, p) if role == 0 else (p, x)

                def send_whole(role=role, ebuf=ebuf, n=n, py=py, px=px, to=to):
                    if n:
                        far(ebuf.at[chunk(c)], fbuf.at[to], gs.at[role, n, 0], fr.at[c, 0], z, py, px, k)
                    else:
                        near(ebuf.at[chunk(c)], fbuf.at[to], fr.at[c, 0])

                def send_halves(role=role, ebuf=ebuf, n=n, py=py, px=px, to=to):
                    if n:
                        for h in range(2):
                            part = pl.ds(h * HALF, HALF)
                            far(
                                ebuf.at[pl.ds(c * PIECE + h * HALF, HALF)], hbuf.at[to, part],
                                gs.at[role, n, h], hr.at[c, 0], z, py, px, h,
                            )
                    else:
                        for h, go in ((k, None), (1 - k, 1 - k)):
                            part = pl.ds(pl.multiple_of(h * HALF, HALF), HALF)
                            here = ebuf.at[pl.ds(pl.multiple_of(c * PIECE + h * HALF, HALF), HALF)]
                            if go is None:
                                near(here, hbuf.at[to, part], hr.at[c, 0])
                            else:
                                far(here, hbuf.at[to, part], gs.at[role, 0, 0], hr.at[c, 0], z, y, x, go)

                pl.when(whole)(send_whole)
                pl.when(halves)(send_halves)

    def gather_sent():
        for role, _, _, _, goals in lines:
            for n, _, whole, halves in goals:

                def sent_whole(role=role, n=n):
                    if n:
                        arrive(fbuf.at[pl.ds(0, PLANES)], gs.at[role, n, 0])

                def sent_halves(role=role, n=n):
                    for h in range(2 if n else 1):
                        arrive(fbuf.at[pl.ds(0, PLANES), pl.ds(0, HALF)], gs.at[role, n, h])

                if n:
                    pl.when(whole)(sent_whole)
                pl.when(halves)(sent_halves)

    f_row = jnp.where(diagonal, k == 0, by_row)
    f_line, f_pos = jnp.where(f_row, y, x), jnp.where(f_row, x, y)
    h_line, h_pos = f_pos, f_line
    f_rel, h_rel = (f_pos - f_line) & 3, (h_pos - h_line) & 3
    f_special = k == jnp.where(f_row, 0, 1)
    h_core = jnp.where(f_row, 0, 1)
    my_half = pl.ds(pl.multiple_of(k * HALF, HALF), HALF)

    def relay(c):
        def f_to(r):
            p = (f_line + r) & 3
            return jnp.where(f_row, y, p), jnp.where(f_row, p, x)

        def h_to(r):
            p = (h_line + r) & 3
            return jnp.where(f_row, p, y), jnp.where(f_row, x, p)

        def whole(s, r, sem):
            if c is None:
                return arrive(fbuf.at[pl.ds(0, PLANES)], vs.at[sem])
            part = fbuf.at[c * SIDE + ((f_line + s) & 3)]
            far(part, part, vs.at[sem], fr.at[c, 1], z, *f_to(r), k)

        def half(s, r, sem, into, arrived, core):
            if c is None:
                return arrive(fbuf.at[pl.ds(0, PLANES), pl.ds(0, HALF)], vs.at[sem])
            at = c * SIDE + ((h_line + s) & 3)
            far(hbuf.at[at, my_half], into.at[at, my_half], vs.at[sem], arrived.at[c, 1], z, *h_to(r), core)

        @pl.when(f_rel == 0)
        def _():
            whole(3, 1, 0)

        @pl.when((f_rel == 1) & f_special)
        def _():
            whole(2, 0, 0)

            @pl.when(f_line < 2)
            def _():
                whole(0, 2, 1)

        @pl.when((f_rel == 2) & jnp.logical_not(f_special))
        def _():
            whole(3, 1, 0)
            for h in range(2):
                if c is None:
                    arrive(fbuf.at[pl.ds(0, PLANES), pl.ds(0, HALF)], vs.at[1 + h])
                else:
                    at, part = c * SIDE + ((f_line + 1) & 3), pl.ds(h * HALF, HALF)
                    far(fbuf.at[at, part], hbuf.at[at, part], vs.at[1 + h], hr.at[c, 1], z, *f_to(3), h)

        @pl.when(across & (h_rel == 2))
        def _():
            half(3, 1, 3, fbuf, fr, h_core)
            half(1, 3, 4, hbuf, hr, k)

        @pl.when(across & (h_rel == 3))
        def _():
            @pl.when(h_line < 2)
            def _():
                half(0, 2, 3, fbuf, fr, h_core)

            @pl.when(h_line >= 2)
            def _():
                half(0, 2, 3, hbuf, hr, k)

    def pass_on(c):
        arrive(fbuf.at[pl.ds(0, 3)], fr.at[c, 0])

        @pl.when(across)
        def _():
            arrive(fbuf.at[pl.ds(0, 3), pl.ds(0, HALF)], hr.at[c, 0])

        relay(c)

    def settle(c):
        arrive(fbuf.at[0], fr.at[c, 1])
        part = pl.ds(c * SIDE, SIDE)

        @pl.when(diagonal)
        def _():
            far(fbuf.at[part], hbuf.at[part], ss, sr.at[c], z, y, x, 1 - k)
            arrive(hbuf.at[part], sr.at[c])

        @pl.when(across)
        def _():
            arrive(fbuf.at[0, pl.ds(0, HALF)], hr.at[c, 1])
            far(hbuf.at[part, my_half], hbuf.at[part, my_half], ss, sr.at[c], z, y, x, 1 - k)
            arrive(fbuf.at[pl.ds(0, SIDE), pl.ds(0, HALF)], sr.at[c])

    for c in range(1, PLANES):
        to = (z - hop(c)) & 3
        far(src.at[chunk(to)], zbuf.at[chunk(c)], zs, zr.at[c], to, y, x, k)
    near(src.at[chunk(z)], zbuf.at[chunk(0)], zr.at[0])
    exchange(0)
    gather(0)
    for ref in (racc, cacc, fcacc, fsend, hsend):
        ref[...] = jnp.full(ref.shape, FLOOR, F32)
    exchange(1)
    exchange(2)
    exchange(3)
    gather(1)
    pass_on(0)
    gather(2)
    pass_on(1)
    gather(3)

    first_slot = jnp.where(f_row, 2 * y, 2 * x) + k
    other_slot = jnp.where(diagonal, 2 * y + 1 - k, jnp.where(by_row, 2 * x, 2 * y + 1))
    together = clus_ref[z * SLOTS + first_slot] == clus_ref[z * SLOTS + other_slot]

    def scores_of(left, i, right, j):
        a = left[pl.ds(i * SIDE, SIDE)].reshape(CHUNK, D)
        b = right[pl.ds(j * SIDE, SIDE)].reshape(CHUNK, D)
        return lax.dot_general(a, b, (((1,), (1,)), ((), ())), preferred_element_type=F32)

    def keep(scores, i, j, col, ok):
        over = scores[:, :128]
        for n in range(1, CHUNK // 128):
            over = jnp.maximum(over, scores[:, n * 128 : (n + 1) * 128])
        down = jnp.max(scores.reshape(CHUNK // 8, 8, CHUNK), axis=0)
        if ok is not None:
            over = jnp.where(ok, over, FLOOR)
            down = jnp.where(ok, down, FLOOR)
        at = pl.ds(i * CHUNK if isinstance(i, int) else pl.multiple_of(i * CHUNK, CHUNK), CHUNK)
        racc[at, :] = jnp.maximum(racc[at, :], over)
        col[j] = jnp.maximum(col[j], down)

    def compute(c):
        @pl.when(diagonal)
        def _():
            def own(t, inner):
                keep(scores_of(fbuf, c, fbuf, t), c, t, fcacc, None)
                return inner

            lax.fori_loop(0, c, own, 0)
            scores = scores_of(fbuf, c, fbuf, c)
            same = lax.broadcasted_iota(I32, scores.shape, 0) == lax.broadcasted_iota(I32, scores.shape, 1)
            keep(jnp.where(same, FLOOR, scores), c, c, fcacc, None)

        def cross(t, inner):
            i = jnp.where(t <= c, c, t - c - 1)
            j = jnp.where(t <= c, t, c)
            wanted = across | ((k == 0) & (i < 2)) | ((k == 1) & (j >= 2))

            @pl.when(wanted)
            def _():
                keep(scores_of(fbuf, i, hbuf, j), i, j, cacc, together)

            return inner

        lax.fori_loop(0, 2 * c + 1, cross, 0)

    def work(c, carry):
        @pl.when(c == 2)
        def _():
            arrive(fbuf.at[pl.ds(0, 3)], zs)
            arrive(fbuf.at[pl.ds(0, 7)], es)
            gather_sent()

        settle(c)
        compute(c)

        @pl.when(c + 2 < PLANES)
        def _():
            pass_on(c + 2)

        return carry

    lax.fori_loop(0, PLANES, work, 0)

    for c in range(PLANES):
        down = jnp.max(cacc[c], axis=0, keepdims=True)
        own = jnp.max(fcacc[c], axis=0, keepdims=True)
        for s in range(SIDE):
            lanes = slice(s * 128, (s + 1) * 128)
            at = c * CHUNK + s * PIECE
            over = jnp.max(racc[at : at + PIECE, :].T, axis=0, keepdims=True)
            fsend[s, c : c + 1, :] = jnp.maximum(over, own[:, lanes])
            hsend[s, c : c + 1, :] = down[:, lanes]

    second = jnp.where(diagonal, 1, k)

    @pl.when(f_row)
    def _():
        core = jnp.where(diagonal, 1, 0)
        for n in range(1, SIDE):
            s, t = (x + n) & 3, (y + n) & 3
            far(fsend.at[s], rrow.at[2 * x], rs, rr.at[0], z, y, s, k)
            far(hsend.at[t], rcol.at[2 * y + second], rs, rr.at[1], z, t, x, core)
        near(fsend.at[x], rrow.at[2 * x], rr.at[0])

        @pl.when(core == k)
        def _():
            near(hsend.at[y], rcol.at[2 * y + second], rr.at[1])

        @pl.when(core != k)
        def _():
            far(hsend.at[y], rcol.at[2 * y + second], ts, rr.at[1], z, y, x, core)

    @pl.when(jnp.logical_not(f_row))
    def _():
        core = jnp.where(diagonal, 0, 1)
        for n in range(1, SIDE):
            s, t = (y + n) & 3, (x + n) & 3
            far(fsend.at[s], rcol.at[2 * y], rs, rr.at[1], z, s, x, k)
            far(hsend.at[t], rrow.at[2 * x + second], rs, rr.at[0], z, y, t, core)
        near(fsend.at[y], rcol.at[2 * y], rr.at[1])

        @pl.when(core == k)
        def _():
            near(hsend.at[x], rrow.at[2 * x + second], rr.at[0])

        @pl.when(core != k)
        def _():
            far(hsend.at[x], rrow.at[2 * x + second], ts, rr.at[0], z, y, x, core)

    for role, (ref, line) in enumerate(((rrow, y), (rcol, x))):
        count = jnp.where(line < 2, 4, jnp.where(k == role, 3, 5))
        for n in (3, 4, 5):

            @pl.when(count == n)
            def _(ref=ref, role=role, n=n):
                arrive(ref.at[pl.ds(0, n)], rr.at[role])

        total = ref[0]
        for i in range(1, 2 * SIDE):
            total = jnp.maximum(total, ref[i])
        ref[0] = total

    for n in range(1, 8):
        i = (in_row + n) & 7
        far(rrow.at[0], brow.at[in_row], bs, br.at[0], z, i // 2, x, i & 1)
        i = (in_col + n) & 7
        far(rcol.at[0], bcol.at[in_col], bs, br.at[1], z, y, i // 2, i & 1)
    near(rrow.at[0], brow.at[in_row], br.at[0])
    near(rcol.at[0], bcol.at[in_col], br.at[1])
    arrive(brow, br.at[0])
    arrive(bcol, br.at[1])
    for c in range(PLANES):
        from_row = jnp.concatenate([brow[s, c : c + 1, :] for s in range(SLOTS)], axis=0)
        from_col = jnp.concatenate([bcol[s, c : c + 1, :] for s in range(SLOTS)], axis=0)
        from_row = pltpu.roll(from_row, (128 - in_row * SHARE) & 127, 1)
        from_col = pltpu.roll(from_col, (128 - in_col * SHARE) & 127, 1)
        value = jnp.maximum(from_row, from_col)
        if c:
            zout[c] = value
            far(zout.at[c], fin.at[c], bs, br.at[2], (z + hop(c)) & 3, y, x, k)
        else:
            fin[0] = value
    arrive(fin.at[pl.ds(1, 3)], br.at[2])

    rows = PLANES * PIECE
    lane = lax.broadcasted_iota(I32, (PIECE, 128), 1)
    sub = lax.broadcasted_iota(I32, (PIECE, 128), 0) & (SHARE - 1)
    best = jnp.full((1, rows), FLOOR, F32)
    for c in range(PLANES):
        spread = jnp.broadcast_to(fin[c].reshape(SLOTS, 1, 128), (SLOTS, SHARE, 128)).reshape(PIECE, 128)
        value = jnp.max(jnp.where(lane == sub, spread, FLOOR), axis=1, keepdims=True)
        pick = ids_ref[chunk((z - hop(c)) & 3), :][:, :1] == lax.broadcasted_iota(I32, (PIECE, rows), 1)
        best = jnp.maximum(best, jnp.max(jnp.where(pick, value, FLOOR), axis=0, keepdims=True))
    out_ref[...] = best

    relay(None)

    @pl.when(diagonal)
    def _():
        arrive(fbuf, ss)

    @pl.when(across)
    def _():
        arrive(fbuf.at[pl.ds(0, 4 * PLANES), pl.ds(0, HALF)], ss)

    arrive(brow.at[pl.ds(0, 6)], rs)

    @pl.when(jnp.where(diagonal, True, k != jnp.where(f_row, 0, 1)))
    def _():
        arrive(brow.at[0], ts)

    arrive(racc.at[pl.ds(0, 17 * 8)], bs)


def by_planes(rows, ids, clus):
    vmem = pl.BlockSpec(memory_space=pltpu.VMEM)
    smem = pl.BlockSpec(memory_space=pltpu.SMEM)
    dma = pltpu.SemaphoreType.DMA
    best = pl.pallas_call(
        plane_kernel,
        out_shape=jax.ShapeDtypeStruct((1, rows.shape[0]), F32),
        in_specs=[smem, vmem, vmem],
        out_specs=vmem,
        scratch_shapes=[
            pltpu.VMEM((PLANES * PIECE, D), BF16),
            pltpu.VMEM((PLANES * PIECE, D), BF16),
            pltpu.VMEM((PLANES * PIECE, D), BF16),
            pltpu.VMEM((PLANES * SIDE, PIECE, D), BF16),
            pltpu.VMEM((PLANES * SIDE, PIECE, D), BF16),
            pltpu.VMEM((PLANES * CHUNK, 128), F32),
            pltpu.VMEM((PLANES, 8, CHUNK), F32),
            pltpu.VMEM((PLANES, 8, CHUNK), F32),
            pltpu.VMEM((SIDE, 8, 128), F32),
            pltpu.VMEM((SIDE, 8, 128), F32),
            pltpu.VMEM((SIDE * 2, 8, 128), F32),
            pltpu.VMEM((SIDE * 2, 8, 128), F32),
            pltpu.VMEM((SLOTS, 8, 128), F32),
            pltpu.VMEM((SLOTS, 8, 128), F32),
            pltpu.VMEM((PLANES, 8, 128), F32),
            pltpu.VMEM((PLANES, 8, 128), F32),
            dma, dma((PLANES,)),
            dma, dma((PLANES,)), dma((PLANES,)),
            dma((2, SIDE, 2)), dma((5,)), dma((PLANES, 2)), dma((PLANES, 2)),
            dma, dma((PLANES,)),
            dma, dma((2,)),
            dma, dma((3,)),
            dma,
        ],
        compiler_params=pltpu.CompilerParams(
            collective_id=0, has_side_effects=True, vmem_limit_bytes=40 * 2**20
        ),
        name="by_planes",
    )(clus, rows, ids)
    return best.reshape(-1)


def shards(embeddings, member_rows, cluster_sizes, unit_pairs):
    rows, ids, clus, fits = prepare(embeddings, member_rows, cluster_sizes)
    return lax.cond(
        fits[0] > 0,
        lambda: by_planes(rows, ids, clus),
        lambda: direct(embeddings, member_rows, cluster_sizes, unit_pairs),
    )


def solution(mesh):
    placed = (P(AXES, None), P(), P(), P())
    return jax.shard_map(shards, mesh=mesh, in_specs=placed, out_specs=P(AXES), check_vma=False)
```

time: 202 us -> 83.4 us (0.41)
  waiting for transfers between devices: 106 us -> 0 us
  Pallas kernels: 0 us -> 81.8 us
  starting transfers between devices: 25.1 us -> 0 us
  matrix products: 23.4 us -> 0 us
  local copies, waits for them, and re-layouts: 22.9 us -> 0.58 us
  other arithmetic: 14.3 us -> 0 us
  loops' own time: 8.44 us -> 0.24 us
    all_to_all x2 -> x0, waiting for transfers between devices: 106 us -> none  [the longest x1 95.9 us: shards(): lax.all_to_all(outgoing, AXES, split_axis=0, concat_axis=0, tiled=True)]
    pallas_call x0 -> x2, Pallas kernels: none -> 81.8 us  [the longest x1 78.5 us: by_planes(): pl.pallas_call(plane_kernel, out_shape=jax.ShapeDtypeStruct((1, rows.shap...]
    all_to_all x2 -> x0, starting transfers between devices: 25.1 us -> none  [the longest x1 13.1 us: shards(): back = lax.all_to_all(best, AXES, split_axis=0, concat_axis=0, tiled=True)]
    dot_general x5 -> x0, matrix products: 23.4 us -> none  [the longest x4 21.4 us: step(): lax.dot_general(part, right, (((1,), (1,)), ((), ())), preferred_element_...]
    gather x2 -> x0, local copies, waits for them, and re-layouts: 9.28 us -> none  [the longest x1 8.6 us: shards(): outgoing = by_group[sides].reshape(owners, 2 * share, width)]
    another operation x1, loops' own time: 8.44 us -> 0.24 us  [shards(): lax.cond(fits[0] > 0, lambda: by_planes(rows, ids, clus), lambda: direct(...]
    slice x1 -> x0, local copies, waits for them, and re-layouts: 6.29 us -> none  [shards(): right = arrived[:, 1].reshape(GROUP, width)]
    gather x2 -> x0, other arithmetic: 4.95 us -> none  [the longest x1 4.94 us: shards(): first_group[jnp.maximum(pairs[:, :1], 0)] + jnp.maximum(pairs[:, 1:], 0)]
  transfers between devices with their start and end apart: 2 -> 0, of which waited for: 2 -> 0; matrix products, arithmetic and copies ran while one was open for 1% -> 0% of each run, Pallas kernels for 0% -> 0%
where the time goes in v3:
time: 83.4 us; the launch traced here: 83.3 us
  Pallas kernels  81.8 us (98%)
    pallas_call x1, Pallas kernels, by_planes(): pl.pallas_call(plane_kernel, out_shape=jax.ShapeDtypeStruct((1, rows.shap...  78.5 us
    pallas_call x1, Pallas kernels, prepare(): pl.pallas_call(functools.partial(prepare_kernel, cluster_sizes.shape[0]),...  3.35 us

profile of v3, /device:TPU:1, one launch (start us, length us, event | category | flops | bytes accessed | tf_op | source)
XLA Modules:
  0.0 83.3 jit_solution(15705968140103124080)
XLA Ops:
  0.0 3.4 %prepare.1 = (bf16[512,1024]{1,0:T(8,128)(2,1)S(1)}, s32[512,128]{1,0:T(8,128)S(1)}, s32[32]{0:T(128)S(1)}, s32[1]{0:T(128)}) custom-call(s32[8]{0:T(128)} %sizes_ref.1, bf16[512,1024]{1,0:T(8,128)(2,1)} %emb_ref.1, s32[512,128]{1,0:T(8,128)} %bitcast.41), custom_call_target="tpu_custom_call" | custom-call | tf_op jit(solution)/shard_map/prepare/pallas_call | solution.py:159
  4.0 78.7 %conditional.1 = (f32[512]{0:T(512)S(1)}) conditional(s32[]{:T(128)} %bitcast.23, (s32[65536]{0:T(1024)}, s32[8]{0:T(128)}, s32[128,1,3]{0,1,2:T(1,128)}, bf16[512,1024]{1,0:T(8,128)(2,1)}) %tuple.15, (s32[32]{0:T(128)S(1)}, bf16[512,1024]{1,0:T(8,128)(2,1)S(1)}, s32[512,128]{1,0:T(8,128)S(1)}) %tuple.16), branch_computations={%region_0.11_spmd, %region_11.12_spmd} | conditional | flops 2695124480 | bytes 68931608 | solution.py:639
  4.0 78.5 %by_planes.1 = f32[1,512]{1,0:T(1,128)S(1)} custom-call(s32[32]{0:T(128)S(1)} %get-tuple-element.64.clus_ref, bf16[512,1024]{1,0:T(8,128)(2,1)S(1)} %get-tuple-element.65.src, s32[512,128]{1,0:T(8,128)S(1)} %get-tuple-element.66.ids_ref), custom_call_target="tpu_custom_call" | custom-call | tf_op jit(solution)/shard_map/cond/branch_1_fun/by_planes/pallas_call | solution.py:599
  82.7 0.6 copy.41

commit v4 on v3

--- a/solution.py
+++ b/solution.py
@@ -181,7 +181,7 @@
     clus_ref, src, ids_ref, out_ref,
     zbuf, erow, ecol, fbuf, hbuf, racc, cacc, fcacc, fsend, hsend,
     rrow, rcol, brow, bcol, zout, fin,
-    zs, zr, es, er, ec, gs, vs, fr, hr, ss, sr,
+    zs, zr, es, er, ec, gs, vs, fr, hr,
     rs, rr, bs, br, ts,
 ):
     z = lax.axis_index("store")
@@ -199,17 +199,8 @@
     def arrive(ref, sem):
         pltpu.make_async_copy(ref, ref, sem).wait()
 
-    def row_first(cy, cx):
-        step = (cx - cy) & 3
-        return (step == 1) | ((step == 2) & (cy < 2))
-
     diagonal = y == x
-    across = jnp.logical_not(diagonal)
-    by_row = row_first(y, x)
     in_row, in_col = 2 * y + k, 2 * x + k
-
-    for ref in (rrow, rcol):
-        ref[...] = jnp.full(ref.shape, FLOOR, F32)
 
     barrier = pltpu.get_barrier_semaphore()
 
@@ -232,12 +223,15 @@
         return pl.ds(c * PIECE if isinstance(c, int) else pl.multiple_of(c * PIECE, PIECE), PIECE)
 
     def exchange(c):
-        arrive(zbuf.at[chunk(c)], zr.at[c])
+        if c:
+            arrive(zbuf.at[chunk(c)], zr.at[c])
         row_at = pl.ds(pl.multiple_of(c * PIECE + in_row * SHARE, SHARE), SHARE)
         col_at = pl.ds(pl.multiple_of(c * PIECE + in_col * SHARE, SHARE), SHARE)
 
         def piece(i):
-            return zbuf.at[pl.ds(pl.multiple_of(c * PIECE + i * SHARE, SHARE), SHARE)]
+            if c:
+                return zbuf.at[pl.ds(pl.multiple_of(c * PIECE + i * SHARE, SHARE), SHARE)]
+            return src.at[pl.ds(pl.multiple_of(z * PIECE + i * SHARE, SHARE), SHARE)]
 
         for n in range(1, 8):
             i = (in_row + n) & 7
@@ -247,163 +241,48 @@
         near(piece(in_row), erow.at[row_at], er.at[c])
         near(piece(in_col), ecol.at[col_at], ec.at[c])
 
-    lines = []
-    for role, (ebuf, esem, line, pos) in enumerate(((erow, er, y, x), (ecol, ec, x, y))):
-        mine = (pos - line) & 3
-        special = k == role
-        wide = line < 2
-        goals = []
-        for n in (1, 3, 0):
-            r = (mine + n) & 3
-            p = (pos + n) & 3
-            whole = (r == 1) | ((r == 2) & wide) | ((r == 0) & special)
-            halves = ((r == 3) | ((r == 2) & jnp.logical_not(wide))) & jnp.logical_not(special)
-            goals.append((n, p, whole, halves))
-        lines.append((role, ebuf, esem, pos, goals))
+    def col_core(cy, member):
+        return jnp.where(cy < x, member, 1 - member)
+
+    member = col_core(y, k)
 
     def gather(c):
-        for role, ebuf, esem, pos, goals in lines:
-            arrive(ebuf.at[chunk(c)], esem.at[c])
-            to = c * SIDE + pos
-            for n, p, whole, halves in goals:
-                py, px = (y, p) if role == 0 else (p, x)
-
-                def send_whole(role=role, ebuf=ebuf, n=n, py=py, px=px, to=to):
-                    if n:
-                        far(ebuf.at[chunk(c)], fbuf.at[to], gs.at[role, n, 0], fr.at[c, 0], z, py, px, k)
-                    else:
-                        near(ebuf.at[chunk(c)], fbuf.at[to], fr.at[c, 0])
-
-                def send_halves(role=role, ebuf=ebuf, n=n, py=py, px=px, to=to):
-                    if n:
-                        for h in range(2):
-                            part = pl.ds(h * HALF, HALF)
-                            far(
-                                ebuf.at[pl.ds(c * PIECE + h * HALF, HALF)], hbuf.at[to, part],
-                                gs.at[role, n, h], hr.at[c, 0], z, py, px, h,
-                            )
-                    else:
-                        for h, go in ((k, None), (1 - k, 1 - k)):
-                            part = pl.ds(pl.multiple_of(h * HALF, HALF), HALF)
-                            here = ebuf.at[pl.ds(pl.multiple_of(c * PIECE + h * HALF, HALF), HALF)]
-                            if go is None:
-                                near(here, hbuf.at[to, part], hr.at[c, 0])
-                            else:
-                                far(here, hbuf.at[to, part], gs.at[role, 0, 0], hr.at[c, 0], z, y, x, go)
-
-                pl.when(whole)(send_whole)
-                pl.when(halves)(send_halves)
-
-    def gather_sent():
-        for role, _, _, _, goals in lines:
-            for n, _, whole, halves in goals:
-
-                def sent_whole(role=role, n=n):
-                    if n:
-                        arrive(fbuf.at[pl.ds(0, PLANES)], gs.at[role, n, 0])
-
-                def sent_halves(role=role, n=n):
-                    for h in range(2 if n else 1):
-                        arrive(fbuf.at[pl.ds(0, PLANES), pl.ds(0, HALF)], gs.at[role, n, h])
-
-                if n:
-                    pl.when(whole)(sent_whole)
-                pl.when(halves)(sent_halves)
-
-    f_row = jnp.where(diagonal, k == 0, by_row)
-    f_line, f_pos = jnp.where(f_row, y, x), jnp.where(f_row, x, y)
-    h_line, h_pos = f_pos, f_line
-    f_rel, h_rel = (f_pos - f_line) & 3, (h_pos - h_line) & 3
-    f_special = k == jnp.where(f_row, 0, 1)
-    h_core = jnp.where(f_row, 0, 1)
-    my_half = pl.ds(pl.multiple_of(k * HALF, HALF), HALF)
-
-    def relay(c):
-        def f_to(r):
-            p = (f_line + r) & 3
-            return jnp.where(f_row, y, p), jnp.where(f_row, p, x)
-
-        def h_to(r):
-            p = (h_line + r) & 3
-            return jnp.where(f_row, p, y), jnp.where(f_row, x, p)
-
-        def whole(s, r, sem):
-            if c is None:
-                return arrive(fbuf.at[pl.ds(0, PLANES)], vs.at[sem])
-            part = fbuf.at[c * SIDE + ((f_line + s) & 3)]
-            far(part, part, vs.at[sem], fr.at[c, 1], z, *f_to(r), k)
-
-        def half(s, r, sem, into, arrived, core):
-            if c is None:
-                return arrive(fbuf.at[pl.ds(0, PLANES), pl.ds(0, HALF)], vs.at[sem])
-            at = c * SIDE + ((h_line + s) & 3)
-            far(hbuf.at[at, my_half], into.at[at, my_half], vs.at[sem], arrived.at[c, 1], z, *h_to(r), core)
-
-        @pl.when(f_rel == 0)
+        arrive(erow.at[chunk(c)], er.at[c])
+        arrive(ecol.at[chunk(c)], ec.at[c])
+        mine, at_row, at_col = chunk(c), c * SIDE + x, c * SIDE + y
+        for way, n in enumerate((1, 3)):
+            px, py = (x + n) & 3, (y + n) & 3
+            far(erow.at[mine], fbuf.at[at_row], gs.at[0], fr.at[c, way], z, y, px, k)
+            far(ecol.at[mine], hbuf.at[at_col], gs.at[0], hr.at[c, way], z, py, x, col_core(py, k))
+        near(erow.at[mine], fbuf.at[at_row], fr.at[c, 2])
+
+        @pl.when(y < x)
         def _():
-            whole(3, 1, 0)
-
-        @pl.when((f_rel == 1) & f_special)
+            near(ecol.at[mine], hbuf.at[at_col], hr.at[c, 2])
+
+        @pl.when(y >= x)
         def _():
-            whole(2, 0, 0)
-
-            @pl.when(f_line < 2)
-            def _():
-                whole(0, 2, 1)
-
-        @pl.when((f_rel == 2) & jnp.logical_not(f_special))
-        def _():
-            whole(3, 1, 0)
-            for h in range(2):
-                if c is None:
-                    arrive(fbuf.at[pl.ds(0, PLANES), pl.ds(0, HALF)], vs.at[1 + h])
-                else:
-                    at, part = c * SIDE + ((f_line + 1) & 3), pl.ds(h * HALF, HALF)
-                    far(fbuf.at[at, part], hbuf.at[at, part], vs.at[1 + h], hr.at[c, 1], z, *f_to(3), h)
-
-        @pl.when(across & (h_rel == 2))
-        def _():
-            half(3, 1, 3, fbuf, fr, h_core)
-            half(1, 3, 4, hbuf, hr, k)
-
-        @pl.when(across & (h_rel == 3))
-        def _():
-            @pl.when(h_line < 2)
-            def _():
-                half(0, 2, 3, fbuf, fr, h_core)
-
-            @pl.when(h_line >= 2)
-            def _():
-                half(0, 2, 3, hbuf, hr, k)
+            far(ecol.at[mine], hbuf.at[at_col], gs.at[1], hr.at[c, 2], z, y, x, 1 - k)
 
     def pass_on(c):
-        arrive(fbuf.at[pl.ds(0, 3)], fr.at[c, 0])
-
-        @pl.when(across)
-        def _():
-            arrive(fbuf.at[pl.ds(0, 3), pl.ds(0, HALF)], hr.at[c, 0])
-
-        relay(c)
+        for way, n in enumerate((1, 3)):
+            part = pl.ds(way * HALF, HALF)
+            px, py = (x + n) & 3, (y + n) & 3
+            at = c * SIDE + ((x - n) & 3)
+            arrive(fbuf.at[at], fr.at[c, way])
+            far(fbuf.at[at, part], fbuf.at[at, part], vs, fr.at[c, 3], z, y, px, k)
+            at = c * SIDE + ((y - n) & 3)
+            arrive(hbuf.at[at], hr.at[c, way])
+            far(hbuf.at[at, part], hbuf.at[at, part], vs, hr.at[c, 3], z, py, x, col_core(py, member))
 
     def settle(c):
-        arrive(fbuf.at[0], fr.at[c, 1])
-        part = pl.ds(c * SIDE, SIDE)
-
-        @pl.when(diagonal)
-        def _():
-            far(fbuf.at[part], hbuf.at[part], ss, sr.at[c], z, y, x, 1 - k)
-            arrive(hbuf.at[part], sr.at[c])
-
-        @pl.when(across)
-        def _():
-            arrive(fbuf.at[0, pl.ds(0, HALF)], hr.at[c, 1])
-            far(hbuf.at[part, my_half], hbuf.at[part, my_half], ss, sr.at[c], z, y, x, 1 - k)
-            arrive(fbuf.at[pl.ds(0, SIDE), pl.ds(0, HALF)], sr.at[c])
+        for sem in (2, 3):
+            arrive(fbuf.at[0], fr.at[c, sem])
+            arrive(hbuf.at[0], hr.at[c, sem])
 
     for c in range(1, PLANES):
         to = (z - hop(c)) & 3
         far(src.at[chunk(to)], zbuf.at[chunk(c)], zs, zr.at[c], to, y, x, k)
-    near(src.at[chunk(z)], zbuf.at[chunk(0)], zr.at[0])
     exchange(0)
     gather(0)
     for ref in (racc, cacc, fcacc, fsend, hsend):
@@ -417,8 +296,8 @@
     pass_on(1)
     gather(3)
 
-    first_slot = jnp.where(f_row, 2 * y, 2 * x) + k
-    other_slot = jnp.where(diagonal, 2 * y + 1 - k, jnp.where(by_row, 2 * x, 2 * y + 1))
+    first_slot = 2 * y + k
+    other_slot = 2 * x + member
     together = clus_ref[z * SLOTS + first_slot] == clus_ref[z * SLOTS + other_slot]
 
     def scores_of(left, i, right, j):
@@ -453,7 +332,7 @@
         def cross(t, inner):
             i = jnp.where(t <= c, c, t - c - 1)
             j = jnp.where(t <= c, t, c)
-            wanted = across | ((k == 0) & (i < 2)) | ((k == 1) & (j >= 2))
+            wanted = jnp.logical_not(diagonal) | (i < j) | ((i == j) & ((k == 0) == (i < 2)))
 
             @pl.when(wanted)
             def _():
@@ -468,7 +347,7 @@
         def _():
             arrive(fbuf.at[pl.ds(0, 3)], zs)
             arrive(fbuf.at[pl.ds(0, 7)], es)
-            gather_sent()
+            arrive(fbuf, gs.at[0])
 
         settle(c)
         compute(c)
@@ -491,52 +370,24 @@
             fsend[s, c : c + 1, :] = jnp.maximum(over, own[:, lanes])
             hsend[s, c : c + 1, :] = down[:, lanes]
 
-    second = jnp.where(diagonal, 1, k)
-
-    @pl.when(f_row)
+    for n in range(1, SIDE):
+        s, t = (x + n) & 3, (y + n) & 3
+        far(fsend.at[s], rrow.at[x], rs, rr.at[0], z, y, s, k)
+        far(hsend.at[t], rcol.at[y], rs, rr.at[1], z, t, x, member)
+    near(fsend.at[x], rrow.at[x], rr.at[0])
+
+    @pl.when(y < x)
     def _():
-        core = jnp.where(diagonal, 1, 0)
-        for n in range(1, SIDE):
-            s, t = (x + n) & 3, (y + n) & 3
-            far(fsend.at[s], rrow.at[2 * x], rs, rr.at[0], z, y, s, k)
-            far(hsend.at[t], rcol.at[2 * y + second], rs, rr.at[1], z, t, x, core)
-        near(fsend.at[x], rrow.at[2 * x], rr.at[0])
-
-        @pl.when(core == k)
-        def _():
-            near(hsend.at[y], rcol.at[2 * y + second], rr.at[1])
-
-        @pl.when(core != k)
-        def _():
-            far(hsend.at[y], rcol.at[2 * y + second], ts, rr.at[1], z, y, x, core)
-
-    @pl.when(jnp.logical_not(f_row))
+        near(hsend.at[y], rcol.at[y], rr.at[1])
+
+    @pl.when(y >= x)
     def _():
-        core = jnp.where(diagonal, 0, 1)
-        for n in range(1, SIDE):
-            s, t = (y + n) & 3, (x + n) & 3
-            far(fsend.at[s], rcol.at[2 * y], rs, rr.at[1], z, s, x, k)
-            far(hsend.at[t], rrow.at[2 * x + second], rs, rr.at[0], z, y, t, core)
-        near(fsend.at[y], rcol.at[2 * y], rr.at[1])
-
-        @pl.when(core == k)
-        def _():
-            near(hsend.at[x], rrow.at[2 * x + second], rr.at[0])
-
-        @pl.when(core != k)
-        def _():
-            far(hsend.at[x], rrow.at[2 * x + second], ts, rr.at[0], z, y, x, core)
-
-    for role, (ref, line) in enumerate(((rrow, y), (rcol, x))):
-        count = jnp.where(line < 2, 4, jnp.where(k == role, 3, 5))
-        for n in (3, 4, 5):
-
-            @pl.when(count == n)
-            def _(ref=ref, role=role, n=n):
-                arrive(ref.at[pl.ds(0, n)], rr.at[role])
-
+        far(hsend.at[y], rcol.at[y], ts, rr.at[1], z, y, x, 1 - k)
+
+    for role, ref in enumerate((rrow, rcol)):
+        arrive(ref, rr.at[role])
         total = ref[0]
-        for i in range(1, 2 * SIDE):
+        for i in range(1, SIDE):
             total = jnp.maximum(total, ref[i])
         ref[0] = total
 
@@ -573,20 +424,12 @@
         best = jnp.maximum(best, jnp.max(jnp.where(pick, value, FLOOR), axis=0, keepdims=True))
     out_ref[...] = best
 
-    relay(None)
-
-    @pl.when(diagonal)
+    arrive(fbuf.at[pl.ds(0, 8)], vs)
+    arrive(brow.at[pl.ds(0, 6)], rs)
+
+    @pl.when(y >= x)
     def _():
-        arrive(fbuf, ss)
-
-    @pl.when(across)
-    def _():
-        arrive(fbuf.at[pl.ds(0, 4 * PLANES), pl.ds(0, HALF)], ss)
-
-    arrive(brow.at[pl.ds(0, 6)], rs)
-
-    @pl.when(jnp.where(diagonal, True, k != jnp.where(f_row, 0, 1)))
-    def _():
+        arrive(fbuf.at[pl.ds(0, PLANES)], gs.at[1])
         arrive(brow.at[0], ts)
 
     arrive(racc.at[pl.ds(0, 17 * 8)], bs)
@@ -612,16 +455,15 @@
             pltpu.VMEM((PLANES, 8, CHUNK), F32),
             pltpu.VMEM((SIDE, 8, 128), F32),
             pltpu.VMEM((SIDE, 8, 128), F32),
-            pltpu.VMEM((SIDE * 2, 8, 128), F32),
-            pltpu.VMEM((SIDE * 2, 8, 128), F32),
+            pltpu.VMEM((SIDE, 8, 128), F32),
+            pltpu.VMEM((SIDE, 8, 128), F32),
             pltpu.VMEM((SLOTS, 8, 128), F32),
             pltpu.VMEM((SLOTS, 8, 128), F32),
             pltpu.VMEM((PLANES, 8, 128), F32),
             pltpu.VMEM((PLANES, 8, 128), F32),
             dma, dma((PLANES,)),
             dma, dma((PLANES,)), dma((PLANES,)),
-            dma((2, SIDE, 2)), dma((5,)), dma((PLANES, 2)), dma((PLANES, 2)),
-            dma, dma((PLANES,)),
+            dma((2,)), dma, dma((PLANES, 4)), dma((PLANES, 4)),
             dma, dma((2,)),
             dma, dma((3,)),
             dma,

time: 83.4 us -> 81.5 us (0.977)
  Pallas kernels: 81.8 us -> 79.9 us
    pallas_call x1, Pallas kernels: 78.5 us -> 76.5 us  [by_planes(): pl.pallas_call(plane_kernel, out_shape=jax.ShapeDtypeStruct((1, rows.shap...]
where the time goes in v4:
time: 81.5 us; the launch traced here: 81.4 us
  Pallas kernels  79.9 us (98%)
    pallas_call x1, Pallas kernels, by_planes(): pl.pallas_call(plane_kernel, out_shape=jax.ShapeDtypeStruct((1, rows.shap...  76.5 us
    pallas_call x1, Pallas kernels, prepare(): pl.pallas_call(functools.partial(prepare_kernel, cluster_sizes.shape[0]),...  3.35 us

profile of v4, /device:TPU:1, one launch (start us, length us, event | category | flops | bytes accessed | tf_op | source)
XLA Modules:
  0.0 81.4 jit_solution(15011061903588898915)
XLA Ops:
  0.0 3.3 %prepare.1 = (bf16[512,1024]{1,0:T(8,128)(2,1)S(1)}, s32[512,128]{1,0:T(8,128)S(1)}, s32[32]{0:T(128)S(1)}, s32[1]{0:T(128)}) custom-call(s32[8]{0:T(128)} %sizes_ref.1, bf16[512,1024]{1,0:T(8,128)(2,1)} %emb_ref.1, s32[512,128]{1,0:T(8,128)} %bitcast.41), custom_call_target="tpu_custom_call" | custom-call | tf_op jit(solution)/shard_map/prepare/pallas_call | solution.py:159
  4.0 76.8 %conditional.1 = (f32[512]{0:T(512)S(1)}) conditional(s32[]{:T(128)} %bitcast.23, (s32[65536]{0:T(1024)}, s32[8]{0:T(128)}, s32[128,1,3]{0,1,2:T(1,128)}, bf16[512,1024]{1,0:T(8,128)(2,1)}) %tuple.15, (s32[32]{0:T(128)S(1)}, bf16[512,1024]{1,0:T(8,128)(2,1)S(1)}, s32[512,128]{1,0:T(8,128)S(1)}) %tuple.16), branch_computations={%region_0.11_spmd, %region_11.12_spmd} | conditional | flops 2695124480 | bytes 68931608 | solution.py:481
  4.0 76.5 %by_planes.1 = f32[1,512]{1,0:T(1,128)S(1)} custom-call(s32[32]{0:T(128)S(1)} %get-tuple-element.64.clus_ref, bf16[512,1024]{1,0:T(8,128)(2,1)S(1)} %get-tuple-element.65.src, s32[512,128]{1,0:T(8,128)S(1)} %get-tuple-element.66.ids_ref), custom_call_target="tpu_custom_call" | custom-call | tf_op jit(solution)/shard_map/cond/branch_1_fun/by_planes/pallas_call | solution.py:442
  80.8 0.6 copy.41

commit v5 on v4

--- a/solution.py
+++ b/solution.py
@@ -178,11 +178,11 @@
 
 
 def plane_kernel(
-    clus_ref, src, ids_ref, out_ref,
-    zbuf, erow, ecol, fbuf, hbuf, racc, cacc, fcacc, fsend, hsend,
+    clus_ref, src, ids_hbm, out_ref,
+    ids_ref, zbuf, erow, ecol, fbuf, hbuf, racc, hacc, cacc, fcacc, fsend, hsend,
     rrow, rcol, brow, bcol, zout, fin,
     zs, zr, es, er, ec, gs, vs, fr, hr,
-    rs, rr, bs, br, ts,
+    rs, rr, bs, br, ts, ids_sem,
 ):
     z = lax.axis_index("store")
     tile = lax.axis_index("tile")
@@ -249,34 +249,33 @@
     def gather(c):
         arrive(erow.at[chunk(c)], er.at[c])
         arrive(ecol.at[chunk(c)], ec.at[c])
-        mine, at_row, at_col = chunk(c), c * SIDE + x, c * SIDE + y
+        mine, at = chunk(c), c * SIDE
         for way, n in enumerate((1, 3)):
             px, py = (x + n) & 3, (y + n) & 3
-            far(erow.at[mine], fbuf.at[at_row], gs.at[0], fr.at[c, way], z, y, px, k)
-            far(ecol.at[mine], hbuf.at[at_col], gs.at[0], hr.at[c, way], z, py, x, col_core(py, k))
-        near(erow.at[mine], fbuf.at[at_row], fr.at[c, 2])
+            far(erow.at[mine], fbuf.at[at + 1 + way], gs.at[0], fr.at[c, way], z, y, px, k)
+            far(ecol.at[mine], hbuf.at[at + 1 + way], gs.at[0], hr.at[c, way], z, py, x, col_core(py, k))
+        near(erow.at[mine], fbuf.at[at], fr.at[c, 2])
 
         @pl.when(y < x)
         def _():
-            near(ecol.at[mine], hbuf.at[at_col], hr.at[c, 2])
+            near(ecol.at[mine], hbuf.at[at], hr.at[c, 2])
 
         @pl.when(y >= x)
         def _():
-            far(ecol.at[mine], hbuf.at[at_col], gs.at[1], hr.at[c, 2], z, y, x, 1 - k)
+            far(ecol.at[mine], hbuf.at[at], gs.at[1], hr.at[c, 2], z, y, x, 1 - k)
 
     def pass_on(c):
         for way, n in enumerate((1, 3)):
             part = pl.ds(way * HALF, HALF)
             px, py = (x + n) & 3, (y + n) & 3
-            at = c * SIDE + ((x - n) & 3)
+            at, to = c * SIDE + 1 + way, c * SIDE + 3
             arrive(fbuf.at[at], fr.at[c, way])
-            far(fbuf.at[at, part], fbuf.at[at, part], vs, fr.at[c, 3], z, y, px, k)
-            at = c * SIDE + ((y - n) & 3)
+            far(fbuf.at[at, part], fbuf.at[to, part], vs, fr.at[c, 3], z, y, px, k)
             arrive(hbuf.at[at], hr.at[c, way])
-            far(hbuf.at[at, part], hbuf.at[at, part], vs, hr.at[c, 3], z, py, x, col_core(py, member))
-
-    def settle(c):
-        for sem in (2, 3):
+            far(hbuf.at[at, part], hbuf.at[to, part], vs, hr.at[c, 3], z, py, x, col_core(py, member))
+
+    def settle(c, shares=(2, 3)):
+        for sem in shares:
             arrive(fbuf.at[0], fr.at[c, sem])
             arrive(hbuf.at[0], hr.at[c, sem])
 
@@ -284,8 +283,9 @@
         to = (z - hop(c)) & 3
         far(src.at[chunk(to)], zbuf.at[chunk(c)], zs, zr.at[c], to, y, x, k)
     exchange(0)
+    near(ids_hbm, ids_ref, ids_sem)
     gather(0)
-    for ref in (racc, cacc, fcacc, fsend, hsend):
+    for ref in (racc, hacc, cacc, fcacc, fsend, hsend):
         ref[...] = jnp.full(ref.shape, FLOOR, F32)
     exchange(1)
     exchange(2)
@@ -294,110 +294,156 @@
     pass_on(0)
     gather(2)
     pass_on(1)
+    pass_on(2)
     gather(3)
 
     first_slot = 2 * y + k
     other_slot = 2 * x + member
     together = clus_ref[z * SLOTS + first_slot] == clus_ref[z * SLOTS + other_slot]
 
-    def scores_of(left, i, right, j):
-        a = left[pl.ds(i * SIDE, SIDE)].reshape(CHUNK, D)
-        b = right[pl.ds(j * SIDE, SIDE)].reshape(CHUNK, D)
-        return lax.dot_general(a, b, (((1,), (1,)), ((), ())), preferred_element_type=F32)
-
-    def keep(scores, i, j, col, ok):
-        over = scores[:, :128]
-        for n in range(1, CHUNK // 128):
-            over = jnp.maximum(over, scores[:, n * 128 : (n + 1) * 128])
-        down = jnp.max(scores.reshape(CHUNK // 8, 8, CHUNK), axis=0)
+    def meet(left, i, rows, right, j, cols, col, ok=None, same=False, rowmax=None):
+        a = left[pl.ds(i, rows)].reshape(rows * PIECE, D)
+        b = right[pl.ds(j, cols)].reshape(cols * PIECE, D)
+        scores = lax.dot_general(a, b, (((1,), (1,)), ((), ())), preferred_element_type=F32)
+        if same:
+            eye = lax.broadcasted_iota(I32, scores.shape, 0) == lax.broadcasted_iota(I32, scores.shape, 1)
+            scores = jnp.where(eye, FLOOR, scores)
+        over = scores[:, :PIECE]
+        for n in range(1, cols):
+            over = jnp.maximum(over, scores[:, n * PIECE : (n + 1) * PIECE])
+        down = jnp.max(scores.reshape(rows * PIECE // 8, 8, cols * PIECE), axis=0)
         if ok is not None:
             over = jnp.where(ok, over, FLOOR)
             down = jnp.where(ok, down, FLOOR)
-        at = pl.ds(i * CHUNK if isinstance(i, int) else pl.multiple_of(i * CHUNK, CHUNK), CHUNK)
-        racc[at, :] = jnp.maximum(racc[at, :], over)
-        col[j] = jnp.maximum(col[j], down)
-
-    def compute(c):
+        at = pl.ds(i * PIECE if isinstance(i, int) else pl.multiple_of(i * PIECE, PIECE), rows * PIECE)
+        if rowmax is None:
+            racc[at, :] = jnp.maximum(racc[at, :], over)
+        else:
+            rowmax[...] = jnp.maximum(rowmax[...], over)
+        for n in range(cols):
+            col[j + n] = jnp.maximum(col[j + n], down[:, n * PIECE : (n + 1) * PIECE])
+
+    off = jnp.logical_not(diagonal)
+
+    def corner(i, rows, t):
         @pl.when(diagonal)
         def _():
-            def own(t, inner):
-                keep(scores_of(fbuf, c, fbuf, t), c, t, fcacc, None)
-                return inner
-
-            lax.fori_loop(0, c, own, 0)
-            scores = scores_of(fbuf, c, fbuf, c)
-            same = lax.broadcasted_iota(I32, scores.shape, 0) == lax.broadcasted_iota(I32, scores.shape, 1)
-            keep(jnp.where(same, FLOOR, scores), c, c, fcacc, None)
-
-        def cross(t, inner):
-            i = jnp.where(t <= c, c, t - c - 1)
-            j = jnp.where(t <= c, t, c)
-            wanted = jnp.logical_not(diagonal) | (i < j) | ((i == j) & ((k == 0) == (i < 2)))
-
-            @pl.when(wanted)
-            def _():
-                keep(scores_of(fbuf, i, hbuf, j), i, j, cacc, together)
-
-            return inner
-
-        lax.fori_loop(0, 2 * c + 1, cross, 0)
-
-    def work(c, carry):
-        @pl.when(c == 2)
+            meet(fbuf, i, rows, fbuf, t * SIDE, SIDE, fcacc)
+
+        @pl.when(off)
         def _():
-            arrive(fbuf.at[pl.ds(0, 3)], zs)
-            arrive(fbuf.at[pl.ds(0, 7)], es)
-            arrive(fbuf, gs.at[0])
-
+            meet(fbuf, i, rows, hbuf, t * SIDE, SIDE, cacc, together)
+
+        meet(fbuf, t * SIDE, SIDE, hbuf, i, rows, cacc, together)
+
+    def middle(i, rows, takes):
+        @pl.when(diagonal)
+        def _():
+            meet(fbuf, i, rows, fbuf, i, rows, fcacc, same=True)
+
+        @pl.when(off | takes)
+        def _():
+            meet(fbuf, i, rows, hbuf, i, rows, cacc, together)
+
+    def compute(c):
+        def before(t, carry):
+            corner(c * SIDE, SIDE, t)
+            return carry
+
+        lax.fori_loop(0, c, before, 0)
+        middle(c * SIDE, SIDE, (k == 0) == (c < 2))
+
+    def early(c, carry):
         settle(c)
         compute(c)
-
-        @pl.when(c + 2 < PLANES)
-        def _():
-            pass_on(c + 2)
-
         return carry
 
-    lax.fori_loop(0, PLANES, work, 0)
-
-    for c in range(PLANES):
-        down = jnp.max(cacc[c], axis=0, keepdims=True)
-        own = jnp.max(fcacc[c], axis=0, keepdims=True)
-        for s in range(SIDE):
-            lanes = slice(s * 128, (s + 1) * 128)
-            at = c * CHUNK + s * PIECE
-            over = jnp.max(racc[at : at + PIECE, :].T, axis=0, keepdims=True)
-            fsend[s, c : c + 1, :] = jnp.maximum(over, own[:, lanes])
-            hsend[s, c : c + 1, :] = down[:, lanes]
-
-    for n in range(1, SIDE):
-        s, t = (x + n) & 3, (y + n) & 3
-        far(fsend.at[s], rrow.at[x], rs, rr.at[0], z, y, s, k)
-        far(hsend.at[t], rcol.at[y], rs, rr.at[1], z, t, x, member)
-    near(fsend.at[x], rrow.at[x], rr.at[0])
+    lax.fori_loop(0, 3, early, 0)
+    pass_on(3)
+    arrive(fbuf.at[pl.ds(0, 3)], zs)
+    arrive(fbuf.at[pl.ds(0, 7)], es)
+    arrive(fbuf, gs.at[0])
+
+    last, takes = 3 * SIDE, k == 1
+    settle(3, (2,))
+
+    def ahead(t, carry):
+        corner(last, 3, t)
+        return carry
+
+    lax.fori_loop(0, 3, ahead, 0)
+    middle(last, 3, takes)
+    def flat(s, c):
+        at = (c * SIDE + s) * PIECE
+        fsend[s, c : c + 1, :] = jnp.max(racc[at : at + PIECE, :].T, axis=0, keepdims=True)
+
+    for s in range(SIDE):
+        for c in range(PLANES):
+            if (s, c) != (3, 3):
+                flat(s, c)
+    settle(3, (3,))
+
+    @pl.when(off)
+    def _():
+        meet(fbuf, 15, 1, hbuf, 0, 16, cacc, together)
+        meet(hbuf, 15, 1, fbuf, 0, 15, fcacc, together, rowmax=hacc)
+
+    @pl.when(diagonal)
+    def _():
+        meet(fbuf, 15, 1, fbuf, 0, 15, fcacc)
+        meet(fbuf, 15, 1, fbuf, 15, 1, fcacc, same=True)
+        meet(hbuf, 15, 1, fbuf, 0, 12, fcacc, together, rowmax=hacc)
+
+    @pl.when(diagonal & takes)
+    def _():
+        meet(fbuf, 15, 1, hbuf, 12, 4, cacc, together)
+        meet(hbuf, 15, 1, fbuf, 12, 3, fcacc, together, rowmax=hacc)
+
+    places = (0, 3, 1, 2)
+    for s in (1, 2, 3, 0):
+        for c in range(PLANES):
+            best = jnp.max(cacc[c * SIDE + s], axis=0, keepdims=True)
+            if (s, c) == (3, 3):
+                best = jnp.maximum(best, jnp.max(hacc[...].T, axis=0, keepdims=True))
+            hsend[s, c : c + 1, :] = best
+        if s:
+            far(hsend.at[s], rcol.at[y], rs, rr.at[1], z, (y + places[s]) & 3, x, member)
 
     @pl.when(y < x)
     def _():
-        near(hsend.at[y], rcol.at[y], rr.at[1])
+        near(hsend.at[0], rcol.at[y], rr.at[1])
 
     @pl.when(y >= x)
     def _():
-        far(hsend.at[y], rcol.at[y], ts, rr.at[1], z, y, x, 1 - k)
-
-    for role, ref in enumerate((rrow, rcol)):
-        arrive(ref, rr.at[role])
-        total = ref[0]
+        far(hsend.at[0], rcol.at[y], ts, rr.at[1], z, y, x, 1 - k)
+
+    flat(3, 3)
+    for s in (1, 2, 3, 0):
+        for c in range(PLANES):
+            best = jnp.max(fcacc[c * SIDE + s], axis=0, keepdims=True)
+            fsend[s, c : c + 1, :] = jnp.maximum(fsend[s, c : c + 1, :], best)
+        if s:
+            far(fsend.at[s], rrow.at[x], rs, rr.at[0], z, y, (x + places[s]) & 3, k)
+        else:
+            near(fsend.at[0], rrow.at[x], rr.at[0])
+
+    def total(ref, sem):
+        arrive(ref, sem)
+        best = ref[0]
         for i in range(1, SIDE):
-            total = jnp.maximum(total, ref[i])
-        ref[0] = total
-
+            best = jnp.maximum(best, ref[i])
+        ref[0] = best
+
+    total(rcol, rr.at[1])
+    for n in range(1, 8):
+        i = (in_col + n) & 7
+        far(rcol.at[0], bcol.at[in_col], bs, br.at[1], z, y, i // 2, i & 1)
+    near(rcol.at[0], bcol.at[in_col], br.at[1])
+    total(rrow, rr.at[0])
     for n in range(1, 8):
         i = (in_row + n) & 7
         far(rrow.at[0], brow.at[in_row], bs, br.at[0], z, i // 2, x, i & 1)
-        i = (in_col + n) & 7
-        far(rcol.at[0], bcol.at[in_col], bs, br.at[1], z, y, i // 2, i & 1)
     near(rrow.at[0], brow.at[in_row], br.at[0])
-    near(rcol.at[0], bcol.at[in_col], br.at[1])
     arrive(brow, br.at[0])
     arrive(bcol, br.at[1])
     for c in range(PLANES):
@@ -413,6 +459,7 @@
             fin[0] = value
     arrive(fin.at[pl.ds(1, 3)], br.at[2])
 
+    arrive(ids_ref, ids_sem)
     rows = PLANES * PIECE
     lane = lax.broadcasted_iota(I32, (PIECE, 128), 1)
     sub = lax.broadcasted_iota(I32, (PIECE, 128), 0) & (SHARE - 1)
@@ -438,21 +485,24 @@
 def by_planes(rows, ids, clus):
     vmem = pl.BlockSpec(memory_space=pltpu.VMEM)
     smem = pl.BlockSpec(memory_space=pltpu.SMEM)
+    anywhere = pl.BlockSpec(memory_space=pl.ANY)
     dma = pltpu.SemaphoreType.DMA
     best = pl.pallas_call(
         plane_kernel,
         out_shape=jax.ShapeDtypeStruct((1, rows.shape[0]), F32),
-        in_specs=[smem, vmem, vmem],
+        in_specs=[smem, vmem, anywhere],
         out_specs=vmem,
         scratch_shapes=[
+            pltpu.VMEM(ids.shape, I32),
             pltpu.VMEM((PLANES * PIECE, D), BF16),
             pltpu.VMEM((PLANES * PIECE, D), BF16),
             pltpu.VMEM((PLANES * PIECE, D), BF16),
             pltpu.VMEM((PLANES * SIDE, PIECE, D), BF16),
             pltpu.VMEM((PLANES * SIDE, PIECE, D), BF16),
             pltpu.VMEM((PLANES * CHUNK, 128), F32),
-            pltpu.VMEM((PLANES, 8, CHUNK), F32),
-            pltpu.VMEM((PLANES, 8, CHUNK), F32),
+            pltpu.VMEM((PIECE, 128), F32),
+            pltpu.VMEM((PLANES * SIDE, 8, PIECE), F32),
+            pltpu.VMEM((PLANES * SIDE, 8, PIECE), F32),
             pltpu.VMEM((SIDE, 8, 128), F32),
             pltpu.VMEM((SIDE, 8, 128), F32),
             pltpu.VMEM((SIDE, 8, 128), F32),
@@ -466,7 +516,7 @@
             dma((2,)), dma, dma((PLANES, 4)), dma((PLANES, 4)),
             dma, dma((2,)),
             dma, dma((3,)),
-            dma,
+            dma, dma,
         ],
         compiler_params=pltpu.CompilerParams(
             collective_id=0, has_side_effects=True, vmem_limit_bytes=40 * 2**20

time: 81.5 us -> 79.4 us (0.974)
  Pallas kernels: 79.9 us -> 77.8 us
    pallas_call x1, Pallas kernels: 76.5 us -> 74.5 us  [by_planes(): pl.pallas_call(plane_kernel, out_shape=jax.ShapeDtypeStruct((1, rows.shap...]
where the time goes in v5:
time: 79.4 us; the launch traced here: 79.3 us
  Pallas kernels  77.8 us (98%)
    pallas_call x1, Pallas kernels, by_planes(): pl.pallas_call(plane_kernel, out_shape=jax.ShapeDtypeStruct((1, rows.shap...  74.5 us
    pallas_call x1, Pallas kernels, prepare(): pl.pallas_call(functools.partial(prepare_kernel, cluster_sizes.shape[0]),...  3.35 us

profile of v5, /device:TPU:1, one launch (start us, length us, event | category | flops | bytes accessed | tf_op | source)
XLA Modules:
  0.0 79.3 jit_solution(12483974015399095692)
XLA Ops:
  0.0 3.3 %prepare.1 = (bf16[512,1024]{1,0:T(8,128)(2,1)S(1)}, s32[512,128]{1,0:T(8,128)S(1)}, s32[32]{0:T(128)S(1)}, s32[1]{0:T(128)}) custom-call(s32[8]{0:T(128)} %sizes_ref.1, bf16[512,1024]{1,0:T(8,128)(2,1)} %emb_ref.1, s32[512,128]{1,0:T(8,128)} %bitcast.41), custom_call_target="tpu_custom_call" | custom-call | tf_op jit(solution)/shard_map/prepare/pallas_call | solution.py:159
  4.0 74.7 %conditional.1 = (f32[512]{0:T(512)S(1)}) conditional(s32[]{:T(128)} %bitcast.23, (s32[65536]{0:T(1024)}, s32[8]{0:T(128)}, s32[128,1,3]{0,1,2:T(1,128)}, bf16[512,1024]{1,0:T(8,128)(2,1)}) %tuple.15, (s32[32]{0:T(128)S(1)}, bf16[512,1024]{1,0:T(8,128)(2,1)S(1)}, s32[512,128]{1,0:T(8,128)S(1)}) %tuple.16), branch_computations={%region_0.11_spmd, %region_11.12_spmd} | conditional | flops 2695124480 | bytes 68931608 | solution.py:531
  4.0 74.5 %by_planes.1 = f32[1,512]{1,0:T(1,128)S(1)} custom-call(s32[32]{0:T(128)S(1)} %get-tuple-element.64.clus_ref, bf16[512,1024]{1,0:T(8,128)(2,1)S(1)} %get-tuple-element.65.src, s32[512,128]{1,0:T(8,128)S(1)} %get-tuple-element.66.ids_hbm), custom_call_target="tpu_custom_call" | custom-call | tf_op jit(solution)/shard_map/cond/branch_1_fun/by_planes/pallas_call | solution.py:490
  78.7 0.6 copy.41

commit v6 on v5

--- a/solution.py
+++ b/solution.py
@@ -444,6 +444,15 @@
         i = (in_row + n) & 7
         far(rrow.at[0], brow.at[in_row], bs, br.at[0], z, i // 2, x, i & 1)
     near(rrow.at[0], brow.at[in_row], br.at[0])
+    arrive(fbuf.at[pl.ds(0, 8)], vs)
+    arrive(racc.at[pl.ds(0, 6 * 8)], rs)
+
+    @pl.when(y >= x)
+    def _():
+        arrive(fbuf.at[pl.ds(0, PLANES)], gs.at[1])
+        arrive(racc.at[pl.ds(0, 8)], ts)
+
+    arrive(ids_ref, ids_sem)
     arrive(brow, br.at[0])
     arrive(bcol, br.at[1])
     for c in range(PLANES):
@@ -457,29 +466,20 @@
             far(zout.at[c], fin.at[c], bs, br.at[2], (z + hop(c)) & 3, y, x, k)
         else:
             fin[0] = value
-    arrive(fin.at[pl.ds(1, 3)], br.at[2])
-
-    arrive(ids_ref, ids_sem)
+
     rows = PLANES * PIECE
     lane = lax.broadcasted_iota(I32, (PIECE, 128), 1)
     sub = lax.broadcasted_iota(I32, (PIECE, 128), 0) & (SHARE - 1)
     best = jnp.full((1, rows), FLOOR, F32)
     for c in range(PLANES):
+        if c == 1:
+            arrive(racc.at[pl.ds(0, 17 * 8)], bs)
+            arrive(fin.at[pl.ds(1, 3)], br.at[2])
         spread = jnp.broadcast_to(fin[c].reshape(SLOTS, 1, 128), (SLOTS, SHARE, 128)).reshape(PIECE, 128)
         value = jnp.max(jnp.where(lane == sub, spread, FLOOR), axis=1, keepdims=True)
         pick = ids_ref[chunk((z - hop(c)) & 3), :][:, :1] == lax.broadcasted_iota(I32, (PIECE, rows), 1)
         best = jnp.maximum(best, jnp.max(jnp.where(pick, value, FLOOR), axis=0, keepdims=True))
     out_ref[...] = best
-
-    arrive(fbuf.at[pl.ds(0, 8)], vs)
-    arrive(brow.at[pl.ds(0, 6)], rs)
-
-    @pl.when(y >= x)
-    def _():
-        arrive(fbuf.at[pl.ds(0, PLANES)], gs.at[1])
-        arrive(brow.at[0], ts)
-
-    arrive(racc.at[pl.ds(0, 17 * 8)], bs)
 
 
 def by_planes(rows, ids, clus):

time: 79.4 us -> 79.4 us (level)
  no operation moved by 1% of the time
where the time goes in v6:
time: 79.4 us; the launch traced here: 79.2 us
  Pallas kernels  77.7 us (98%)
    pallas_call x1, Pallas kernels, by_planes(): pl.pallas_call(plane_kernel, out_shape=jax.ShapeDtypeStruct((1, rows.shap...  74.4 us
    pallas_call x1, Pallas kernels, prepare(): pl.pallas_call(functools.partial(prepare_kernel, cluster_sizes.shape[0]),...  3.35 us

profile of v6, /device:TPU:1, one launch (start us, length us, event | category | flops | bytes accessed | tf_op | source)
XLA Modules:
  0.0 79.2 jit_solution(4125473052083057035)
XLA Ops:
  0.0 3.4 %prepare.1 = (bf16[512,1024]{1,0:T(8,128)(2,1)S(1)}, s32[512,128]{1,0:T(8,128)S(1)}, s32[32]{0:T(128)S(1)}, s32[1]{0:T(128)}) custom-call(s32[8]{0:T(128)} %sizes_ref.1, bf16[512,1024]{1,0:T(8,128)(2,1)} %emb_ref.1, s32[512,128]{1,0:T(8,128)} %bitcast.41), custom_call_target="tpu_custom_call" | custom-call | tf_op jit(solution)/shard_map/prepare/pallas_call | solution.py:159
  4.0 74.6 %conditional.1 = (f32[512]{0:T(512)S(1)}) conditional(s32[]{:T(128)} %bitcast.23, (s32[65536]{0:T(1024)}, s32[8]{0:T(128)}, s32[128,1,3]{0,1,2:T(1,128)}, bf16[512,1024]{1,0:T(8,128)(2,1)}) %tuple.15, (s32[32]{0:T(128)S(1)}, bf16[512,1024]{1,0:T(8,128)(2,1)S(1)}, s32[512,128]{1,0:T(8,128)S(1)}) %tuple.16), branch_computations={%region_0.11_spmd, %region_11.12_spmd} | conditional | flops 2695124480 | bytes 68931608 | solution.py:531
  4.0 74.4 %by_planes.1 = f32[1,512]{1,0:T(1,128)S(1)} custom-call(s32[32]{0:T(128)S(1)} %get-tuple-element.64.clus_ref, bf16[512,1024]{1,0:T(8,128)(2,1)S(1)} %get-tuple-element.65.src, s32[512,128]{1,0:T(8,128)S(1)} %get-tuple-element.66.ids_hbm), custom_call_target="tpu_custom_call" | custom-call | tf_op jit(solution)/shard_map/cond/branch_1_fun/by_planes/pallas_call | solution.py:490
  78.6 0.6 copy.41

commit v7 on v6

--- a/solution.py
+++ b/solution.py
@@ -291,8 +291,8 @@
     exchange(2)
     exchange(3)
     gather(1)
+    gather(2)
     pass_on(0)
-    gather(2)
     pass_on(1)
     pass_on(2)
     gather(3)

time: 79.4 us -> 79.4 us (level)
  no operation moved by 1% of the time
where the time goes in v7:
time: 79.4 us; the launch traced here: 79.2 us
  Pallas kernels  77.7 us (98%)
    pallas_call x1, Pallas kernels, by_planes(): pl.pallas_call(plane_kernel, out_shape=jax.ShapeDtypeStruct((1, rows.shap...  74.4 us
    pallas_call x1, Pallas kernels, prepare(): pl.pallas_call(functools.partial(prepare_kernel, cluster_sizes.shape[0]),...  3.35 us

profile of v7, /device:TPU:1, one launch (start us, length us, event | category | flops | bytes accessed | tf_op | source)
XLA Modules:
  0.0 79.2 jit_solution(17176316265956956028)
XLA Ops:
  0.0 3.3 %prepare.1 = (bf16[512,1024]{1,0:T(8,128)(2,1)S(1)}, s32[512,128]{1,0:T(8,128)S(1)}, s32[32]{0:T(128)S(1)}, s32[1]{0:T(128)}) custom-call(s32[8]{0:T(128)} %sizes_ref.1, bf16[512,1024]{1,0:T(8,128)(2,1)} %emb_ref.1, s32[512,128]{1,0:T(8,128)} %bitcast.41), custom_call_target="tpu_custom_call" | custom-call | tf_op jit(solution)/shard_map/prepare/pallas_call | solution.py:159
  4.0 74.6 %conditional.1 = (f32[512]{0:T(512)S(1)}) conditional(s32[]{:T(128)} %bitcast.23, (s32[65536]{0:T(1024)}, s32[8]{0:T(128)}, s32[128,1,3]{0,1,2:T(1,128)}, bf16[512,1024]{1,0:T(8,128)(2,1)}) %tuple.15, (s32[32]{0:T(128)S(1)}, bf16[512,1024]{1,0:T(8,128)(2,1)S(1)}, s32[512,128]{1,0:T(8,128)S(1)}) %tuple.16), branch_computations={%region_0.11_spmd, %region_11.12_spmd} | conditional | flops 2695124480 | bytes 68931608 | solution.py:531
  4.0 74.4 %by_planes.1 = f32[1,512]{1,0:T(1,128)S(1)} custom-call(s32[32]{0:T(128)S(1)} %get-tuple-element.64.clus_ref, bf16[512,1024]{1,0:T(8,128)(2,1)S(1)} %get-tuple-element.65.src, s32[512,128]{1,0:T(8,128)S(1)} %get-tuple-element.66.ids_hbm), custom_call_target="tpu_custom_call" | custom-call | tf_op jit(solution)/shard_map/cond/branch_1_fun/by_planes/pallas_call | solution.py:490
  78.6 0.6 copy.41
